TPU v7x, 32 devices: a whole 2x2x4 slice. The times are simulated.
32 devices in a mesh: groups: 2 (over x), tp: 16 (over z, y, core).
Axes of the slice: x: 2, y: 2, z: 4, core: 2. Of those that a mesh axis runs over, the one named last changes fastest.
Arguments:
- tokens: bfloat16 [64, 8192], P(('groups', 'tp')), parts along dimension 0, may hold values from -6 to 6
- norm_gain_vector: float32 [8192], replicated, may hold values from 0.1 to 1.9
- query_weight: bfloat16 [8192, 2048], P(None, 'tp'), may hold values from -0.0625 to 0.0625
- key_value_weight: bfloat16 [8192, 2048], P(None, 'tp'), may hold values from -0.0625 to 0.0625
- output_weight: bfloat16 [2048, 8192], P('tp'), may hold values from -0.125 to 0.125
- adapter_down_factor: bfloat16 [32, 8192, 64], P(('groups', 'tp')), parts along dimension 0, may hold values from -0.0625 to 0.0625
- adapter_up_factor: bfloat16 [32, 64, 2048], P(('groups', 'tp')), parts along dimension 0, may hold values from -0.75 to 0.75
- cached_key_rows: bfloat16 [64, 128, 1024], P(('groups', 'tp')), parts along dimension 0, may hold values from -100 to 100
- cached_value_rows: bfloat16 [64, 128, 1024], P(('groups', 'tp')), parts along dimension 0, may hold values from -6 to 6
- row_adapter_index: int32 [64], P('groups'), parts along dimension 0, may hold values from 0 to 15
- cached_length_rows: int32 [64], P(('groups', 'tp')), parts along dimension 0, may hold values from 1 to 128, as said below
- adapter_slot_index: int32 [32], P('groups'), parts along dimension 0, may hold values from 0 to 15, each once
Outputs:
- attn_out: bfloat16 [64, 8192], P(('groups', 'tp')), parts along dimension 0
There are 2 independent parts, one for each index of `groups`. A program takes and returns all parts, laid end to end along the dimension named above; an argument that names none is the same for every part. Nothing has to cross between parts.
Inputs may be any that keep to these rules, and one draw needn't show every extreme that they name: Each slot appears once; adapter a is stored at index adapter_slot_index[a] of adapter_down_factor and adapter_up_factor. `cached_length_rows`: some row has exactly 128 cached positions.
All inputs are finite; a program needn't handle non-finite values.
Results may differ from a plain program's by a relative error of at most 0.0085.
The roundings to bfloat16 on the way count: a program that leaves them out, or rounds other values in their place, can miss the bound.
Values may be sent and summed in bfloat16 or wider, within the bound.
A program may use at most 64 MiB of HBM per device.

v0:
```python
import math

import jax
import jax.numpy as jnp
from jax import lax
from jax.sharding import PartitionSpec as P

KV_HEADS = 8
HEAD_WIDTH = 128


EPSILON = 1e-05
ADAPTER_SCALE = 0.5
ROPE_BASE = 500000.0


def rotate(values_in, places):
    half_size = HEAD_WIDTH // 2
    freqs = ROPE_BASE ** (-jnp.arange(half_size, dtype=jnp.float32) / half_size)
    angles = places.astype(jnp.float32)[:, None, None] * freqs[None, None, :]
    cosine = jnp.cos(angles)
    sine = jnp.sin(angles)
    first_half = values_in[..., :half_size]
    second_half = values_in[..., half_size:]
    return jnp.concatenate(
        [first_half * cosine - second_half * sine, second_half * cosine + first_half * sine],
        axis=-1,
    )


def attend(query_vector, keyval, cached_key_rows, cached_value_rows, lengths_here):
    row_count = query_vector.shape[0]
    head_count = query_vector.shape[1] // HEAD_WIDTH
    group_size = head_count // KV_HEADS
    kv_width = KV_HEADS * HEAD_WIDTH
    queries = rotate(
        query_vector.astype(jnp.float32).reshape(row_count, head_count, HEAD_WIDTH), lengths_here
    ).astype(jnp.bfloat16)
    new_keys = rotate(
        keyval[:, :kv_width].astype(jnp.float32).reshape(row_count, KV_HEADS, HEAD_WIDTH),
        lengths_here,
    ).astype(jnp.bfloat16)
    new_values = keyval[:, kv_width:].reshape(row_count, KV_HEADS, HEAD_WIDTH)
    grouped = queries.reshape(row_count, KV_HEADS, group_size, HEAD_WIDTH)
    old_keys = cached_key_rows.reshape(row_count, -1, KV_HEADS, HEAD_WIDTH)
    old_values = cached_value_rows.reshape(row_count, -1, KV_HEADS, HEAD_WIDTH)
    factor = 1.0 / math.sqrt(HEAD_WIDTH)
    scores = (
        jnp.einsum("rgqd,rcgd->rgqc", grouped, old_keys, preferred_element_type=jnp.float32)
        * factor
    )
    own_score = (
        jnp.einsum("rgqd,rgd->rgq", grouped, new_keys, preferred_element_type=jnp.float32) * factor
    )
    valid = jnp.arange(old_keys.shape[1], dtype=jnp.int32)[None, :] < lengths_here[:, None]
    scores = jnp.where(valid[:, None, None, :], scores, -jnp.inf)
    highest = jnp.maximum(jnp.max(scores, axis=-1), own_score)
    expos = jnp.exp(scores - highest[..., None])
    own_expo = jnp.exp(own_score - highest)
    total = jnp.sum(expos, axis=-1) + own_expo
    weights = (expos / total[..., None]).astype(jnp.bfloat16)
    own_weight = (own_expo / total).astype(jnp.bfloat16)
    context = jnp.einsum("rgqc,rcgd->rgqd", weights, old_values, preferred_element_type=jnp.float32)
    context = (
        context
        + own_weight.astype(jnp.float32)[..., None] * new_values.astype(jnp.float32)[:, :, None, :]
    )
    return context.astype(jnp.bfloat16).reshape(row_count, head_count * HEAD_WIDTH)


def on_device(
    tokens,
    norm_gain_vector,
    query_weight,
    key_value_weight,
    output_weight,
    adapter_down_factor,
    adapter_up_factor,
    cached_key_rows,
    cached_value_rows,
    row_adapter_index,
    cached_length_rows,
    adapter_slot_index,
):
    position = lax.axis_index("tp")
    widened = tokens.astype(jnp.float32)
    normalized_input = (
        widened
        * lax.rsqrt(jnp.mean(widened * widened, axis=-1, keepdims=True) + EPSILON)
        * norm_gain_vector
    ).astype(jnp.bfloat16)
    adapter_count = adapter_slot_index.shape[0]
    resident_count = adapter_down_factor.shape[0]
    rank_width = adapter_down_factor.shape[2]
    hidden_width = adapter_down_factor.shape[1]
    table = row_adapter_index[:, None] == jnp.arange(adapter_count, dtype=jnp.int32)[None, :]
    slot = jnp.sum(jnp.where(table, adapter_slot_index[None, :], 0), axis=1)
    local_slots = position * resident_count + jnp.arange(resident_count, dtype=jnp.int32)
    owned = slot[:, None] == local_slots[None, :]
    down_factor_rows = jnp.transpose(adapter_down_factor, (1, 0, 2)).reshape(
        hidden_width, resident_count * rank_width
    )
    query_cols = query_weight.shape[1]
    kv_cols = key_value_weight.shape[1]
    piece = lax.all_gather(normalized_input, "tp", axis=0, tiled=True)
    piece_rows = piece.shape[0]
    query_part = jnp.dot(piece, query_weight, preferred_element_type=jnp.float32)
    kv_part = jnp.dot(piece, key_value_weight, preferred_element_type=jnp.float32)
    low_part = jnp.dot(piece, down_factor_rows, preferred_element_type=jnp.float32).reshape(
        piece_rows, resident_count, rank_width
    )
    low_part = jnp.sum(jnp.where(owned[:, :, None], low_part, 0.0), axis=1)
    whole = jnp.concatenate([query_part, kv_part, low_part], axis=1)
    plain_query = whole[:, :query_cols]
    keyval = whole[:, query_cols : query_cols + kv_cols].astype(jnp.bfloat16)
    low_term = whole[:, query_cols + kv_cols :]
    low = lax.psum(low_term, "tp").astype(jnp.bfloat16)
    row_total = low.shape[0]
    masked_low = jnp.where(owned[:, :, None], low[:, None, :], jnp.zeros((), jnp.bfloat16)).reshape(
        row_total, resident_count * rank_width
    )
    up_factor_rows = adapter_up_factor.reshape(
        resident_count * rank_width, adapter_up_factor.shape[2]
    )
    terms = lax.psum_scatter(
        lax.dot_general(
            up_factor_rows, masked_low, (((0,), (1,)), ((), ())), preferred_element_type=jnp.float32
        ),
        "tp",
        scatter_dimension=0,
        tiled=True,
    )
    query_correction = jnp.transpose(terms)
    query_vector = (plain_query + ADAPTER_SCALE * query_correction).astype(jnp.bfloat16)
    row_query, row_keyval = (
        lax.all_to_all(query_vector, "tp", split_axis=0, concat_axis=1, tiled=True),
        lax.all_to_all(keyval, "tp", split_axis=0, concat_axis=1, tiled=True),
    )
    context = attend(row_query, row_keyval, cached_key_rows, cached_value_rows, cached_length_rows)
    head_context = lax.all_to_all(context, "tp", split_axis=1, concat_axis=0, tiled=True)
    summed = lax.psum_scatter(
        jnp.dot(head_context, output_weight, preferred_element_type=jnp.float32),
        "tp",
        scatter_dimension=0,
        tiled=True,
    )
    return summed.astype(jnp.bfloat16)


def solution(mesh):
    in_specs = (
        P(("groups", "tp"), None),
        P(),
        P(None, "tp"),
        P(None, "tp"),
        P("tp", None),
        P(("groups", "tp"), None, None),
        P(("groups", "tp"), None, None),
        P(("groups", "tp"), None, None),
        P(("groups", "tp"), None, None),
        P("groups"),
        P(("groups", "tp")),
        P("groups"),
    )
    out_specs = P(("groups", "tp"), None)
    return jax.shard_map(
        on_device, mesh=mesh, in_specs=in_specs, out_specs=out_specs, check_vma=False
    )
```

profile of v0, /device:TPU:0, one launch (start us, length us, event | category | flops | bytes accessed | tf_op | source)
XLA Modules:
  0.0 261.1 jit_solution(7955727066517349061)
XLA Ops:
  6.5 1.1 fusion.9
  7.6 0.9 fusion.12
  8.5 24.6 %all-gather = bf16[16,2,8192]{2,1,0:T(2,128)(2,1)S(1)} all-gather(bf16[1,2,8192]{2,1,0:T(2,128)(2,1)S(1)} %fusion.12), channel_id=1, replica_groups=mesh['groups'=2,'tp'=16] {'tp'}, dimensions={0}, use_global_device_ids=true | all-gather | bytes 557056 | tf_op jit(solution)/shard_map/all_gather | solution.py:105
  33.1 0.2 reshape.157
  33.4 2.7 %convolution_convert_fusion = bf16[32,128]{1,0:T(8,128)(2,1)} fusion(bf16[32,8192]{1,0:T(8,128)(2,1)S(1)} %reshape.157, bf16[8192,128]{1,0:T(8,128)(2,1)} %param.15), kind=kOutput, calls=%fused_computation.8 | convolution fusion | flops 67112960 | bytes 2629632 | tf_op jit(solution)/shard_map/dot_general | solution.py:108
  36.0 3.5 %all-to-all-start.1 = ((bf16[16,2,128]{2,1,0:T(2,128)(2,1)}), bf16[16,2,128]{2,1,0:T(2,128)(2,1)S(1)}, u32[]{:S(2)}, u32[]{:S(2)}) async-start(bf16[16,2,128]{2,1,0:T(2,128)(2,1)} %bitcast.9), calls=%async_computation.2 | async-start | bytes 16384 | tf_op jit(solution)/shard_map/all_to_all | solution.py:137
  39.5 0.0 reduce-scatter.2.cloned.1.call-start
  39.6 0.1 select_reduce_fusion
  39.7 1.6 convolution_select_fusion
  41.3 62.0 %psum.7 = bf16[32,64]{1,0:T(8,128)(2,1)S(1)} all-reduce(f32[32,64]{1,0:T(8,128)S(1)} %convolution_select_fusion), channel_id=1, replica_groups=mesh['groups'=2,'tp'=16] {'tp'}, use_global_device_ids=true, to_apply=%region_2.3 | all-reduce | flops 2048 | bytes 12288 | tf_op jit(solution)/shard_map/psum | solution.py:117
  103.3 0.9 convolution_bitcast_fusion
  104.2 0.0 reduce-scatter.2.cloned.1.call-update
  104.3 0.1 multiply_cosine_fusion
  104.4 0.1 iota_compare_fusion.1
  104.5 0.1 subtract_convert_fusion.1
  104.6 52.4 %reduce-scatter.2.cloned.1.call-done = f32[128,32]{0,1:T(8,128)} async-done(((f32[2048,32]{0,1:T(8,128)}), f32[128,32]{0,1:T(8,128)}) %reduce-scatter.2.cloned.1.call-update) | async-done | bytes 16400 | tf_op jit(solution)/shard_map/reduce_scatter | solution.py:125
  157.0 2.6 %fusion.1 = bf16[32,128]{1,0:T(8,128)(2,1)} fusion(bf16[32,8192]{1,0:T(8,128)(2,1)S(1)} %reshape.157, bf16[8192,128]{1,0:T(8,128)(2,1)} %param.14, f32[128,32]{0,1:T(8,128)} %reduce-scatter.2.cloned.1.call-done), kind=kOutput, calls=%fused_computation.6 | convolution fusion | flops 67121152 | bytes 2646016 | tf_op jit(solution)/shard_map/dot_general | solution.py:107
  159.7 3.7 %all-to-all-start = ((bf16[16,2,128]{2,1,0:T(2,128)(2,1)}), bf16[16,2,128]{2,1,0:T(2,128)(2,1)S(1)}, u32[]{:S(2)}, u32[]{:S(2)}) async-start(bf16[16,2,128]{2,1,0:T(2,128)(2,1)} %bitcast.5), calls=%async_computation.1 | async-start | bytes 16384 | tf_op jit(solution)/shard_map/all_to_all | solution.py:136
  163.4 0.1 maximum_bitcast_fusion
  163.5 6.3 %all-to-all-done = bf16[16,2,128]{2,1,0:T(2,128)(2,1)S(1)} async-done(((bf16[16,2,128]{2,1,0:T(2,128)(2,1)}), bf16[16,2,128]{2,1,0:T(2,128)(2,1)S(1)}, u32[]{:S(2)}, u32[]{:S(2)}) %all-to-all-start) | async-done | bytes 8224 | tf_op jit(solution)/shard_map/all_to_all | solution.py:136
  169.7 0.1 subtract_convert_fusion
  169.9 0.2 fusion.19
  170.1 0.5 fusion.25
  170.6 0.2 fusion.13
  170.8 1.3 fusion.2
  172.1 0.6 copy.31
  172.8 3.5 %all-to-all-start.2 = ((bf16[2,16,128]{2,0,1:T(2,128)(2,1)}), bf16[2,16,128]{2,0,1:T(2,128)(2,1)S(1)}, u32[]{:S(2)}, u32[]{:S(2)}) async-start(bf16[2,16,128]{2,0,1:T(2,128)(2,1)} %copy.31), calls=%async_computation.3 | async-start | bytes 16384 | tf_op jit(solution)/shard_map/all_to_all | solution.py:140
  176.2 0.6 dynamic-slice
  177.5 5.0 %all-to-all-done.2 = bf16[2,16,128]{2,0,1:T(2,128)(2,1)S(1)} async-done(((bf16[2,16,128]{2,0,1:T(2,128)(2,1)}), bf16[2,16,128]{2,0,1:T(2,128)(2,1)S(1)}, u32[]{:S(2)}, u32[]{:S(2)}) %all-to-all-start.2) | async-done | bytes 8224 | tf_op jit(solution)/shard_map/all_to_all | solution.py:140
  182.5 0.4 fusion.26
  182.9 69.8 %all-reduce.2 = bf16[32,8192]{1,0:T(8,128)(2,1)} all-reduce(f32[32,8192]{1,0:T(8,128)S(1)} %fusion.26), channel_id=3, replica_groups=mesh['groups'=2,'tp'=16] {'tp'}, use_global_device_ids=true, to_apply=%region_6.7.clone | all-reduce | flops 262144 | bytes 1572864
  252.7 1.6 dynamic-slice_convert_fusion
  (26 shorter events, 0.1 us)
Async XLA Ops:
  6.5 176.0 %copy-start = (bf16[128,8192]{1,0:T(8,128)(2,1)S(1)}, bf16[128,8192]{1,0:T(8,128)(2,1)}, u32[]{:S(2)}) copy-start(bf16[128,8192]{1,0:T(8,128)(2,1)} %param.16) | copy-start | bytes 6291460
  8.5 31.0 %copy-start.3 = (s32[16]{0:T(128)S(1)}, s32[16]{0:T(128)}, u32[]{:S(2)}) copy-start(s32[16]{0:T(128)} %param.23) | copy-start | bytes 196
  8.5 31.0 %copy-start.4 = (s32[32]{0:T(128)S(1)}, s32[32]{0:T(128)}, u32[]{:S(2)}) copy-start(s32[32]{0:T(128)} %param.21) | copy-start | bytes 388
  33.3 70.0 %copy-start.1 = (bf16[1,64,2048]{2,1,0:T(8,128)(2,1)S(1)}, bf16[1,64,2048]{2,1,0:T(8,128)(2,1)}, u32[]{:S(2)}) copy-start(bf16[1,64,2048]{2,1,0:T(8,128)(2,1)} %param.18) | copy-start | bytes 786436
  33.3 70.9 %copy-start.5 = (s32[2]{0:T(128)S(1)}, s32[2]{0:T(128)}, u32[]{:S(2)}) copy-start(s32[2]{0:T(128)} %param.22) | copy-start | bytes 28
  36.0 68.4 %all-to-all-start.1 = ((bf16[16,2,128]{2,1,0:T(2,128)(2,1)}), bf16[16,2,128]{2,1,0:T(2,128)(2,1)S(1)}, u32[]{:S(2)}, u32[]{:S(2)}) async-start(bf16[16,2,128]{2,1,0:T(2,128)(2,1)} %bitcast.9), calls=%async_computation.2 | async-start | bytes 16384 | tf_op jit(solution)/shard_map/all_to_all | solution.py:137
  39.5 117.5 %reduce-scatter.2.cloned.1.call-start = ((), (), s32[]{:S(2)}) async-start(), calls=%async_computation.4 | async-start | bytes 278528 | tf_op jit(solution)/shard_map/reduce_scatter | solution.py:125
  41.3 128.8 %copy-start.2 = (bf16[2,128,1024]{2,1,0:T(8,128)(2,1)S(1)}, bf16[2,128,1024]{2,1,0:T(8,128)(2,1)}, u32[]{:S(2)}) copy-start(bf16[2,128,1024]{2,1,0:T(8,128)(2,1)} %param.19) | copy-start | bytes 1572868
  104.6 71.7 %copy-start.6 = (u32[32]{0:T(128)S(1)}, u32[32]{0:T(128)}, u32[]{:S(2)}) copy-start(u32[32]{0:T(128)} %constant.35) | copy-start | bytes 388
  159.7 10.1 %all-to-all-start = ((bf16[16,2,128]{2,1,0:T(2,128)(2,1)}), bf16[16,2,128]{2,1,0:T(2,128)(2,1)S(1)}, u32[]{:S(2)}, u32[]{:S(2)}) async-start(bf16[16,2,128]{2,1,0:T(2,128)(2,1)} %bitcast.5), calls=%async_computation.1 | async-start | bytes 16384 | tf_op jit(solution)/shard_map/all_to_all | solution.py:136
  172.8 9.8 %all-to-all-start.2 = ((bf16[2,16,128]{2,0,1:T(2,128)(2,1)}), bf16[2,16,128]{2,0,1:T(2,128)(2,1)S(1)}, u32[]{:S(2)}, u32[]{:S(2)}) async-start(bf16[2,16,128]{2,0,1:T(2,128)(2,1)} %copy.31), calls=%async_computation.3 | async-start | bytes 16384 | tf_op jit(solution)/shard_map/all_to_all | solution.py:140
Sparse Core Ops, SparseCore 0:
  104.4 52.5 reduce-scatter.1
where the time goes:
time: 262 us; the launch traced here: 261 us
  blocking collectives  156 us (60%)
  waiting for transfers between devices  63.7 us (24%)
  between operations  14.2 us (5%)
  starting transfers between devices  10.7 us (4%)
  matrix products  10.3 us (4%)
  local copies, waits for them, and re-layouts  3.07 us (1%)
  other arithmetic  2.73 us (1%)
    unnamed x1, blocking collectives  69.8 us
    psum x1, blocking collectives, on_device(): low = lax.psum(low_term, 'tp').astype(jnp.bfloat16)  62 us
    reduce_scatter x1, waiting for transfers between devices, on_device(): lax.psum_scatter(lax.dot_general(up_factor_rows, masked_low, (((0,), (1,)...  52.4 us
    all_gather x1, blocking collectives, on_device(): piece = lax.all_gather(normalized_input, 'tp', axis=0, tiled=True)  24.6 us
    all_to_all x1, waiting for transfers between devices, on_device(): lax.all_to_all(query_vector, 'tp', split_axis=0, concat_axis=1, tiled=True)  6.25 us
  transfers between devices with their start and end apart: 4, of which 3 were waited for; matrix products, arithmetic and copies ran while one was open for 1% of the time, Pallas kernels for 0%

commit v1 on v0

--- a/solution.py
+++ b/solution.py
@@ -1,8 +1,11 @@
+import functools
 import math
 
 import jax
 import jax.numpy as jnp
 from jax import lax
+from jax.experimental import pallas as pl
+from jax.experimental.pallas import tpu as pltpu
 from jax.sharding import PartitionSpec as P
 
 KV_HEADS = 8
@@ -12,6 +15,175 @@
 EPSILON = 1e-05
 ADAPTER_SCALE = 0.5
 ROPE_BASE = 500000.0
+
+VMEM_LIMIT = 24 * 1024 * 1024
+CHUNKS = 4
+FOLD = 8
+
+
+def peers(n):
+    me = lax.axis_index("tp")
+    outer = n // 4
+    a, b, c = me // 4, (me // 2) % 2, me % 2
+    core_peer = a * 4 + b * 2 + (1 - c)
+    mid_peer = a * 4 + (1 - b) * 2 + c
+    ahead = [((a + k) % outer) * 4 + b * 2 + c for k in range(outer)]
+    behind = [((a + outer - k) % outer) * 4 + b * 2 + c for k in range(outer)]
+    return me, outer, a, b, c, core_peer, mid_peer, ahead, behind
+
+
+def greet(partners):
+    barrier = pltpu.get_barrier_semaphore()
+    for partner in partners:
+        pl.semaphore_signal(
+            barrier, inc=1, device_id={"tp": partner}, device_id_type=pl.DeviceIdType.MESH
+        )
+    pl.semaphore_wait(barrier, len(partners))
+
+
+def send(src, dst, send_sem, recv_sem, target):
+    return pltpu.make_async_remote_copy(
+        src_ref=src,
+        dst_ref=dst,
+        send_sem=send_sem,
+        recv_sem=recv_sem,
+        device_id={"tp": target},
+        device_id_type=pl.DeviceIdType.MESH,
+    )
+
+
+def gather_kernel(n, width, x_ref, gain_ref, out_ref, far_send, mid_send, core_send, recv):
+    me, outer, a, b, c, core_peer, mid_peer, ahead, behind = peers(n)
+    rows = x_ref.shape[0] // FOLD
+    for r in range(rows):
+        part = pl.ds(r * FOLD, FOLD)
+        x = x_ref[part, :].astype(jnp.float32)
+        mean = jnp.sum(x * x) / width
+        out_ref[me, part, :] = (x * lax.rsqrt(mean + EPSILON) * gain_ref[...]).astype(jnp.bfloat16)
+    greet([core_peer, mid_peer] + ahead[1:])
+
+    def push(block, sem, target):
+        copy = send(out_ref.at[block], out_ref.at[block], sem, recv.at[block], target)
+        copy.start()
+        return copy
+
+    def arrived(block):
+        send(out_ref.at[block], out_ref.at[block], core_send.at[0], recv.at[block], core_peer).wait_recv()
+
+    copies = [push(me, far_send.at[k], ahead[k]) for k in range(1, outer)]
+    copies.append(push(me, mid_send.at[0], mid_peer))
+    copies.append(push(me, core_send.at[0], core_peer))
+    for k in range(1, outer):
+        arrived(behind[k])
+        copies.append(push(behind[k], mid_send.at[k], mid_peer))
+        copies.append(push(behind[k], core_send.at[k], core_peer))
+    across = [behind[k] - b * 2 + (1 - b) * 2 for k in range(outer)]
+    for k in range(outer):
+        arrived(across[k])
+        copies.append(push(across[k], core_send.at[outer + k], core_peer))
+    for k in range(outer):
+        arrived(behind[k] - c + (1 - c))
+    for k in range(outer):
+        arrived(across[k] - c + (1 - c))
+    for copy in copies:
+        copy.wait_send()
+
+
+def normalize_and_gather(tokens, gain, n):
+    rows, width = tokens.shape
+    fold_width = width // FOLD
+    outer = n // 4
+    gathered = pl.pallas_call(
+        functools.partial(gather_kernel, n, width),
+        out_shape=jax.ShapeDtypeStruct((n, rows * FOLD, fold_width), jnp.bfloat16),
+        in_specs=[pl.BlockSpec(memory_space=pltpu.VMEM)] * 2,
+        out_specs=pl.BlockSpec(memory_space=pltpu.VMEM),
+        scratch_shapes=[
+            pltpu.SemaphoreType.DMA((outer,)),
+            pltpu.SemaphoreType.DMA((outer,)),
+            pltpu.SemaphoreType.DMA((2 * outer,)),
+            pltpu.SemaphoreType.DMA((n,)),
+        ],
+        compiler_params=pltpu.CompilerParams(
+            collective_id=0, has_side_effects=True, vmem_limit_bytes=VMEM_LIMIT
+        ),
+    )(tokens.reshape(rows * FOLD, fold_width), gain.reshape(FOLD, fold_width))
+    return gathered.reshape(n * rows, width)
+
+
+def project_kernel(
+    n, rows, ctx_ref, w_ref, out_ref, p_ref, r1, r2, x_ref, r3, s1, q1, s2, q2, s3, q3
+):
+    me, outer, a, b, c, core_peer, mid_peer, ahead, behind = peers(n)
+    cols = w_ref.shape[1] // CHUNKS
+    quarter = outer * rows
+    greet([core_peer, mid_peer] + ahead[1:])
+    first, second, third = [], [], []
+    for i in range(CHUNKS):
+        part = jnp.dot(
+            ctx_ref[...], w_ref[:, i * cols : (i + 1) * cols], preferred_element_type=jnp.float32
+        )
+        p_ref[i] = part.reshape(2, 2, quarter, cols)
+        copy = send(p_ref.at[i, 1 - c], r1.at[i], s1.at[i], q1.at[i], core_peer)
+        copy.start()
+        first.append(copy)
+    for i in range(CHUNKS):
+        first[i].wait()
+        p_ref[i, c] = p_ref[i, c] + r1[i]
+        copy = send(p_ref.at[i, c, 1 - b], r2.at[i], s2.at[i], q2.at[i], mid_peer)
+        copy.start()
+        second.append(copy)
+    for i in range(CHUNKS):
+        second[i].wait()
+        both = p_ref[i, c, b] + r2[i]
+        for t in range(outer):
+            x_ref[i, t] = both[t * rows : (t + 1) * rows, :]
+        group = []
+        for k in range(1, outer):
+            copy = send(
+                x_ref.at[i, (a + k) % outer], r3.at[i, k], s3.at[i, k], q3.at[i, k], ahead[k]
+            )
+            copy.start()
+            group.append(copy)
+        third.append(group)
+    for i in range(CHUNKS):
+        total = x_ref[i, a]
+        for k in range(1, outer):
+            third[i][k - 1].wait()
+            total = total + r3[i, k]
+        out_ref[:, i * cols : (i + 1) * cols] = total.astype(jnp.bfloat16)
+
+
+def project_and_scatter(head_context, weight, n):
+    total_rows, depth = head_context.shape
+    rows = total_rows // n
+    outer = n // 4
+    width = weight.shape[1]
+    cols = width // CHUNKS
+    quarter = outer * rows
+    ordered = jnp.transpose(head_context.reshape(outer, 2, 2, rows, depth), (2, 1, 0, 3, 4))
+    return pl.pallas_call(
+        functools.partial(project_kernel, n, rows),
+        out_shape=jax.ShapeDtypeStruct((rows, width), jnp.bfloat16),
+        in_specs=[pl.BlockSpec(memory_space=pltpu.VMEM)] * 2,
+        out_specs=pl.BlockSpec(memory_space=pltpu.VMEM),
+        scratch_shapes=[
+            pltpu.VMEM((CHUNKS, 2, 2, quarter, cols), jnp.float32),
+            pltpu.VMEM((CHUNKS, 2, quarter, cols), jnp.float32),
+            pltpu.VMEM((CHUNKS, quarter, cols), jnp.float32),
+            pltpu.VMEM((CHUNKS, outer, rows, cols), jnp.float32),
+            pltpu.VMEM((CHUNKS, outer, rows, cols), jnp.float32),
+            pltpu.SemaphoreType.DMA((CHUNKS,)),
+            pltpu.SemaphoreType.DMA((CHUNKS,)),
+            pltpu.SemaphoreType.DMA((CHUNKS,)),
+            pltpu.SemaphoreType.DMA((CHUNKS,)),
+            pltpu.SemaphoreType.DMA((CHUNKS, outer)),
+            pltpu.SemaphoreType.DMA((CHUNKS, outer)),
+        ],
+        compiler_params=pltpu.CompilerParams(
+            collective_id=1, has_side_effects=True, vmem_limit_bytes=VMEM_LIMIT
+        ),
+    )(ordered.reshape(total_rows, depth), weight)
 
 
 def rotate(values_in, places):
@@ -83,12 +255,7 @@
     adapter_slot_index,
 ):
     position = lax.axis_index("tp")
-    widened = tokens.astype(jnp.float32)
-    normalized_input = (
-        widened
-        * lax.rsqrt(jnp.mean(widened * widened, axis=-1, keepdims=True) + EPSILON)
-        * norm_gain_vector
-    ).astype(jnp.bfloat16)
+    tp = lax.axis_size("tp")
     adapter_count = adapter_slot_index.shape[0]
     resident_count = adapter_down_factor.shape[0]
     rank_width = adapter_down_factor.shape[2]
@@ -102,49 +269,38 @@
     )
     query_cols = query_weight.shape[1]
     kv_cols = key_value_weight.shape[1]
-    piece = lax.all_gather(normalized_input, "tp", axis=0, tiled=True)
+    piece = normalize_and_gather(tokens, norm_gain_vector, tp)
     piece_rows = piece.shape[0]
     query_part = jnp.dot(piece, query_weight, preferred_element_type=jnp.float32)
     kv_part = jnp.dot(piece, key_value_weight, preferred_element_type=jnp.float32)
     low_part = jnp.dot(piece, down_factor_rows, preferred_element_type=jnp.float32).reshape(
         piece_rows, resident_count, rank_width
     )
-    low_part = jnp.sum(jnp.where(owned[:, :, None], low_part, 0.0), axis=1)
-    whole = jnp.concatenate([query_part, kv_part, low_part], axis=1)
-    plain_query = whole[:, :query_cols]
-    keyval = whole[:, query_cols : query_cols + kv_cols].astype(jnp.bfloat16)
-    low_term = whole[:, query_cols + kv_cols :]
-    low = lax.psum(low_term, "tp").astype(jnp.bfloat16)
-    row_total = low.shape[0]
-    masked_low = jnp.where(owned[:, :, None], low[:, None, :], jnp.zeros((), jnp.bfloat16)).reshape(
-        row_total, resident_count * rank_width
+    low = low_part.astype(jnp.bfloat16)
+    masked_low = jnp.where(owned[:, :, None], low, jnp.zeros((), jnp.bfloat16)).reshape(
+        piece_rows, resident_count * rank_width
     )
     up_factor_rows = adapter_up_factor.reshape(
         resident_count * rank_width, adapter_up_factor.shape[2]
     )
-    terms = lax.psum_scatter(
-        lax.dot_general(
-            up_factor_rows, masked_low, (((0,), (1,)), ((), ())), preferred_element_type=jnp.float32
-        ),
-        "tp",
-        scatter_dimension=0,
-        tiled=True,
-    )
-    query_correction = jnp.transpose(terms)
-    query_vector = (plain_query + ADAPTER_SCALE * query_correction).astype(jnp.bfloat16)
-    row_query, row_keyval = (
-        lax.all_to_all(query_vector, "tp", split_axis=0, concat_axis=1, tiled=True),
-        lax.all_to_all(keyval, "tp", split_axis=0, concat_axis=1, tiled=True),
+    terms = jnp.dot(masked_low, up_factor_rows, preferred_element_type=jnp.float32)
+    packed = jnp.concatenate([query_part, kv_part, terms], axis=1)
+    packed = packed.reshape(tp, piece_rows // tp, packed.shape[1])
+    received = lax.all_to_all(packed, "tp", split_axis=0, concat_axis=0, tiled=True)
+    own_rows = piece_rows // tp
+    plain_query = jnp.transpose(received[:, :, :query_cols], (1, 0, 2)).reshape(own_rows, -1)
+    row_keyval = (
+        jnp.transpose(received[:, :, query_cols : query_cols + kv_cols], (1, 0, 2))
+        .reshape(own_rows, -1)
+    )
+    row_keyval = lax.reduce_precision(row_keyval, 8, 7).astype(jnp.bfloat16)
+    correction = jnp.sum(received[:, :, query_cols + kv_cols :], axis=0)
+    row_query = lax.reduce_precision(plain_query + ADAPTER_SCALE * correction, 8, 7).astype(
+        jnp.bfloat16
     )
     context = attend(row_query, row_keyval, cached_key_rows, cached_value_rows, cached_length_rows)
     head_context = lax.all_to_all(context, "tp", split_axis=1, concat_axis=0, tiled=True)
-    summed = lax.psum_scatter(
-        jnp.dot(head_context, output_weight, preferred_element_type=jnp.float32),
-        "tp",
-        scatter_dimension=0,
-        tiled=True,
-    )
-    return summed.astype(jnp.bfloat16)
+    return project_and_scatter(head_context, output_weight, tp)
 
 
 def solution(mesh):

time: 262 us -> 63.3 us (0.24)
  blocking collectives: 156 us -> 9.32 us
  waiting for transfers between devices: 63.7 us -> 10.4 us
  Pallas kernels: 0 us -> 28.2 us
  between operations: 14.2 us -> 0.25 us
  starting transfers between devices: 10.7 us -> 4.53 us
  matrix products: 10.3 us -> 4.79 us
    unnamed x1 -> x0, blocking collectives: 69.8 us -> none
    psum x1 -> x0, blocking collectives: 62 us -> none  [on_device(): low = lax.psum(low_term, 'tp').astype(jnp.bfloat16)]
    reduce_scatter x1 -> x0, waiting for transfers between devices: 52.4 us -> none  [on_device(): lax.psum_scatter(lax.dot_general(up_factor_rows, masked_low, (((0,), (1,)...]
    pallas_call x0 -> x2, Pallas kernels: none -> 28.2 us  [the longest x1 14.6 us: project_and_scatter(): pl.pallas_call(functools.partial(project_kernel, n, rows), out_shape=jax....]
    all_gather x1 -> x0, blocking collectives: 24.6 us -> none  [on_device(): piece = lax.all_gather(normalized_input, 'tp', axis=0, tiled=True)]
    all_to_all x0 -> x1, blocking collectives: none -> 9.32 us  [on_device(): lax.all_to_all(context, 'tp', split_axis=1, concat_axis=0, tiled=True)]
    all_to_all x3 -> x1, starting transfers between devices: 10.7 us -> 4.53 us  [on_device(): lax.all_to_all(packed, 'tp', split_axis=0, concat_axis=0, tiled=True)]
    reshape x0 -> x4, local copies, waits for them, and re-layouts: none -> 2.82 us  [the longest x1 0.93 us: normalize_and_gather(): tokens.reshape(rows * FOLD, fold_width)]
  transfers between devices with their start and end apart: 4 -> 1, of which waited for: 3 -> 1; matrix products, arithmetic and copies ran while one was open for 1% -> 0% of each run, Pallas kernels for 0% -> 0%
where the time goes in v1:
time: 63.3 us; the launch traced here: 63 us
  Pallas kernels  28.2 us (45%)
  waiting for transfers between devices  10.4 us (16%)
  blocking collectives  9.32 us (15%)
  matrix products  4.79 us (8%)
  local copies, waits for them, and re-layouts  4.61 us (7%)
  starting transfers between devices  4.53 us (7%)
  other arithmetic  0.86 us (1%)
    pallas_call x1, Pallas kernels, project_and_scatter(): pl.pallas_call(functools.partial(project_kernel, n, rows), out_shape=jax....  14.6 us
    pallas_call x1, Pallas kernels, normalize_and_gather(): pl.pallas_call(functools.partial(gather_kernel, n, width), out_shape=jax....  13.6 us
    all_to_all x1, waiting for transfers between devices, on_device(): lax.all_to_all(packed, 'tp', split_axis=0, concat_axis=0, tiled=True)  10.4 us
    all_to_all x1, blocking collectives, on_device(): lax.all_to_all(context, 'tp', split_axis=1, concat_axis=0, tiled=True)  9.32 us
    all_to_all x1, starting transfers between devices, on_device(): lax.all_to_all(packed, 'tp', split_axis=0, concat_axis=0, tiled=True)  4.53 us
    dot_general x1, matrix products, on_device(): jnp.dot(masked_low, up_factor_rows, preferred_element_type=jnp.float32)  1.83 us
    unnamed x17, local copies, waits for them, and re-layouts  1.76 us
    dot_general x1, matrix products, attend(): jnp.einsum('rgqd,rcgd->rgqc', grouped, old_keys, preferred_element_type=j...  1.57 us
  transfers between devices with their start and end apart: 1, of which 1 were waited for; matrix products, arithmetic and copies ran while one was open for 0% of the time, Pallas kernels for 0%

profile of v1, /device:TPU:0, one launch (start us, length us, event | category | flops | bytes accessed | tf_op | source)
XLA Modules:
  0.0 63.0 jit_solution(7183122539873248643)
XLA Ops:
  0.0 0.9 %reshape.157.x_ref = bf16[16,1024]{1,0:T(8,128)(2,1)S(1)} reshape(bf16[2,8192]{1,0:T(2,128)(2,1)} %param.12) | data formatting | bytes 65536 | tf_op jit(solution)/shard_map/reshape | solution.py:110
  0.9 0.8 %reshape.158.gain_ref = f32[8,1024]{1,0:T(8,128)S(1)} reshape(f32[8192]{0:T(1024)} %param.13) | data formatting | bytes 65536 | tf_op jit(solution)/shard_map/reshape | solution.py:110
  1.7 13.6 %shard_map.118 = bf16[16,16,1024]{2,1,0:T(8,128)(2,1)S(1)} custom-call(bf16[16,1024]{1,0:T(8,128)(2,1)S(1)} %reshape.157.x_ref, f32[8,1024]{1,0:T(8,128)S(1)} %reshape.158.gain_ref), custom_call_target="tpu_custom_call" | custom-call | tf_op jit(solution)/shard_map/pallas_call | solution.py:96
  15.3 0.2 reshape.159
  15.6 0.0 copy-done
  15.6 0.0 copy-start.2
  15.6 0.0 copy-start.5
  15.6 0.0 copy-start.6
  15.6 0.0 copy-start.3
  15.6 0.4 fusion.28
  16.1 1.1 %copy-done.2 = bf16[8192,128]{1,0:T(8,128)(2,1)S(1)} copy-done((bf16[8192,128]{1,0:T(8,128)(2,1)S(1)}, bf16[8192,128]{1,0:T(8,128)(2,1)}, u32[]{:S(2)}) %copy-start.2) | copy-done | bytes 2097176
  17.2 0.4 fusion.29
  17.7 0.0 copy-start.7
  17.7 0.1 select_reduce_fusion
  17.8 1.8 %fusion.3 = f32[32,2048]{1,0:T(8,128)S(1)} fusion(bf16[32,8192]{1,0:T(8,128)(2,1)S(1)} %reshape.159, bf16[1,8192,64]{1,2,0:T(8,128)(2,1)} %param.17, bf16[1,64,2048]{2,1,0:T(8,128)(2,1)S(1)} %copy-done.3, pred[32]{0:T(512)(128)(4,1)S(1)} %broadcast_compare_fusion), kind=kOutput, calls=%fused_computation.6 | convolution fusion | flops 41947136 | bytes 2097184 | tf_op jit(solution)/shard_map/dot_general | solution.py:286
  19.6 0.0 copy-start.4
  19.6 0.9 %reshape.161 = f32[16,2,2304]{2,1,0:T(2,128)} reshape(f32[32,2304]{1,0:T(8,128)S(1)} %pad_maximum_fusion) | data formatting | bytes 589824 | tf_op jit(solution)/shard_map/reshape | solution.py:288
  20.5 4.5 %all-to-all-start = ((f32[16,2,2304]{2,1,0:T(2,128)}), f32[16,2,2304]{2,1,0:T(2,128)S(1)}, u32[]{:S(2)}, u32[]{:S(2)}) async-start(f32[16,2,2304]{2,1,0:T(2,128)} %reshape.161), calls=%async_computation | async-start | bytes 589824 | tf_op jit(solution)/shard_map/all_to_all | solution.py:289
  25.1 0.1 iota_compare_fusion.1
  25.2 0.1 multiply_cosine_fusion
  25.3 10.4 %all-to-all-done = f32[16,2,2304]{2,1,0:T(2,128)S(1)} async-done(((f32[16,2,2304]{2,1,0:T(2,128)}), f32[16,2,2304]{2,1,0:T(2,128)S(1)}, u32[]{:S(2)}, u32[]{:S(2)}) %all-to-all-start) | async-done | bytes 294944 | tf_op jit(solution)/shard_map/all_to_all | solution.py:289
  35.7 0.1 subtract_convert_fusion.1
  35.8 0.1 slice_reduce_fusion
  35.8 0.1 subtract_convert_fusion
  36.0 0.1 maximum_bitcast_fusion
  36.0 0.2 fusion.21
  36.2 1.6 %fusion.27 = (f32[2,8,2]{2,1,0:T(8,128)S(1)}, f32[2,8,2,128]{3,2,1,0:T(2,128)S(1)}) fusion(bf16[2,8,2,64]{3,2,1,0:T(2,128)(2,1)S(1)} %bitcast.74, bf16[2,8,2,64]{3,2,1,0:T(2,128)(2,1)S(1)} %bitcast.72, pred[2,128]{1,0:T(4,128)(4,1)S(1)} %iota_compare_fusion.1, bf16[2,128,1024]{2,1,0:T(8,128)(2,1)} %param.19), kind=kOutput, calls=%fused_computation.55 | convolution fusion | flops 1077216 | bytes 549248 | tf_op jit(solution)/shard_map/rgqd,rcgd->rgqc/dot_general | solution.py:221
  37.8 0.2 fusion.15
  38.1 0.3 fusion.1
  38.4 9.3 %all_to_all.21 = bf16[2,16,128]{2,0,1:T(2,128)(2,1)S(1)} all-to-all(bf16[2,16,128]{2,0,1:T(2,128)(2,1)S(1)} %copy.33), channel_id=1, replica_groups=mesh['groups'=2,'tp'=16] {'tp'}, dimensions={1} | all-to-all | bytes 16384 | tf_op jit(solution)/shard_map/all_to_all | solution.py:302
  47.7 14.6 %shard_map.119 = bf16[2,8192]{1,0:T(2,128)(2,1)S(1)} custom-call(bf16[32,128]{1,0:T(8,128)(2,1)S(1)} %bitcast.67, bf16[128,8192]{1,0:T(8,128)(2,1)S(1)} %copy-done.1), custom_call_target="tpu_custom_call" | custom-call | tf_op jit(solution)/shard_map/pallas_call | solution.py:165
  62.3 0.6 copy.57
  (23 shorter events, 0.2 us)
Async XLA Ops:
  0.0 15.6 %copy-start = (bf16[8192,128]{1,0:T(8,128)(2,1)S(1)}, bf16[8192,128]{1,0:T(8,128)(2,1)}, u32[]{:S(2)}) copy-start(bf16[8192,128]{1,0:T(8,128)(2,1)} %param.14) | copy-start | bytes 6291460
  15.6 1.6 %copy-start.2 = (bf16[8192,128]{1,0:T(8,128)(2,1)S(1)}, bf16[8192,128]{1,0:T(8,128)(2,1)}, u32[]{:S(2)}) copy-start(bf16[8192,128]{1,0:T(8,128)(2,1)} %param.15) | copy-start | bytes 6291460
  15.6 2.0 %copy-start.5 = (s32[16]{0:T(128)S(1)}, s32[16]{0:T(128)}, u32[]{:S(2)}) copy-start(s32[16]{0:T(128)} %param.23) | copy-start | bytes 196
  15.6 2.0 %copy-start.6 = (s32[32]{0:T(128)S(1)}, s32[32]{0:T(128)}, u32[]{:S(2)}) copy-start(s32[32]{0:T(128)} %param.21) | copy-start | bytes 388
  15.6 2.1 %copy-start.3 = (bf16[1,64,2048]{2,1,0:T(8,128)(2,1)S(1)}, bf16[1,64,2048]{2,1,0:T(8,128)(2,1)}, u32[]{:S(2)}) copy-start(bf16[1,64,2048]{2,1,0:T(8,128)(2,1)} %param.18) | copy-start | bytes 786436
  17.7 7.4 %copy-start.7 = (s32[2]{0:T(128)S(1)}, s32[2]{0:T(128)}, u32[]{:S(2)}) copy-start(s32[2]{0:T(128)} %param.22) | copy-start | bytes 28
  19.6 18.4 %copy-start.4 = (bf16[2,128,1024]{2,1,0:T(8,128)(2,1)S(1)}, bf16[2,128,1024]{2,1,0:T(8,128)(2,1)}, u32[]{:S(2)}) copy-start(bf16[2,128,1024]{2,1,0:T(8,128)(2,1)} %param.20) | copy-start | bytes 1572868
  20.5 15.1 %all-to-all-start = ((f32[16,2,2304]{2,1,0:T(2,128)}), f32[16,2,2304]{2,1,0:T(2,128)S(1)}, u32[]{:S(2)}, u32[]{:S(2)}) async-start(f32[16,2,2304]{2,1,0:T(2,128)} %reshape.161), calls=%async_computation | async-start | bytes 589824 | tf_op jit(solution)/shard_map/all_to_all | solution.py:289
  35.6 12.1 %copy-start.1 = (bf16[128,8192]{1,0:T(8,128)(2,1)S(1)}, bf16[128,8192]{1,0:T(8,128)(2,1)}, u32[]{:S(2)}) copy-start(bf16[128,8192]{1,0:T(8,128)(2,1)} %w_ref.1) | copy-start | bytes 6291460

commit v2 on v1

--- a/solution.py
+++ b/solution.py
@@ -111,17 +111,93 @@
     return gathered.reshape(n * rows, width)
 
 
+def others(n):
+    me = lax.axis_index("tp")
+    return me, [(me + k) % n for k in range(1, n)], [(me + n - k) % n for k in range(1, n)]
+
+
+def exchange_kernel(n, packed_ref, out_ref, own_sem, send_sem, recv_sem):
+    me, to, origin = others(n)
+    own = pltpu.make_async_copy(packed_ref.at[me], out_ref.at[me], own_sem)
+    own.start()
+    greet(to)
+    copies = []
+    for k in range(n - 1):
+        copy = send(
+            packed_ref.at[to[k]], out_ref.at[me], send_sem.at[k], recv_sem.at[k], to[k]
+        )
+        copy.start()
+        copies.append(copy)
+    own.wait()
+    for k in range(n - 1):
+        copies[k].wait_send()
+        send(
+            packed_ref.at[to[k]], out_ref.at[origin[k]], send_sem.at[k], recv_sem.at[k], to[k]
+        ).wait_recv()
+
+
+def exchange(packed, n):
+    return pl.pallas_call(
+        functools.partial(exchange_kernel, n),
+        out_shape=jax.ShapeDtypeStruct(packed.shape, packed.dtype),
+        in_specs=[pl.BlockSpec(memory_space=pltpu.VMEM)],
+        out_specs=pl.BlockSpec(memory_space=pltpu.VMEM),
+        scratch_shapes=[
+            pltpu.SemaphoreType.DMA(()),
+            pltpu.SemaphoreType.DMA((n - 1,)),
+            pltpu.SemaphoreType.DMA((n - 1,)),
+        ],
+        compiler_params=pltpu.CompilerParams(
+            collective_id=2, has_side_effects=True, vmem_limit_bytes=VMEM_LIMIT
+        ),
+    )(packed)
+
+
 def project_kernel(
-    n, rows, ctx_ref, w_ref, out_ref, p_ref, r1, r2, x_ref, r3, s1, q1, s2, q2, s3, q3
+    n,
+    rows,
+    heads_ref,
+    w_ref,
+    out_ref,
+    h_ref,
+    ctx_ref,
+    p_ref,
+    r1,
+    r2,
+    x_ref,
+    r3,
+    s0,
+    q0,
+    s1,
+    q1,
+    s2,
+    q2,
+    s3,
+    q3,
 ):
     me, outer, a, b, c, core_peer, mid_peer, ahead, behind = peers(n)
     cols = w_ref.shape[1] // CHUNKS
     quarter = outer * rows
-    greet([core_peer, mid_peer] + ahead[1:])
+    slot = (c * 2 + b) * outer + a
+    _, to, _ = others(n)
+    greet(to)
+    sent = []
+    for k in range(n - 1):
+        copy = send(heads_ref.at[to[k]], h_ref.at[slot], s0.at[k], q0.at[slot], to[k])
+        copy.start()
+        sent.append(copy)
+    h_ref[slot] = heads_ref[me]
+    for k in range(n - 1):
+        source = (me + n - 1 - k) % n
+        place = ((source % 2) * 2 + (source // 2) % 2) * outer + source // 4
+        send(heads_ref.at[to[k]], h_ref.at[place], s0.at[k], q0.at[place], to[k]).wait_recv()
+    for t in range(n):
+        ctx_ref[t * rows : (t + 1) * rows, :] = h_ref[t]
+    context = ctx_ref[...].astype(jnp.bfloat16)
     first, second, third = [], [], []
     for i in range(CHUNKS):
         part = jnp.dot(
-            ctx_ref[...], w_ref[:, i * cols : (i + 1) * cols], preferred_element_type=jnp.float32
+            context, w_ref[:, i * cols : (i + 1) * cols], preferred_element_type=jnp.float32
         )
         p_ref[i] = part.reshape(2, 2, quarter, cols)
         copy = send(p_ref.at[i, 1 - c], r1.at[i], s1.at[i], q1.at[i], core_peer)
@@ -152,27 +228,31 @@
             third[i][k - 1].wait()
             total = total + r3[i, k]
         out_ref[:, i * cols : (i + 1) * cols] = total.astype(jnp.bfloat16)
-
-
-def project_and_scatter(head_context, weight, n):
-    total_rows, depth = head_context.shape
-    rows = total_rows // n
+    for copy in sent:
+        copy.wait_send()
+
+
+def project_and_scatter(heads, weight, n):
+    rows, depth = heads.shape[1:]
     outer = n // 4
     width = weight.shape[1]
     cols = width // CHUNKS
     quarter = outer * rows
-    ordered = jnp.transpose(head_context.reshape(outer, 2, 2, rows, depth), (2, 1, 0, 3, 4))
     return pl.pallas_call(
         functools.partial(project_kernel, n, rows),
         out_shape=jax.ShapeDtypeStruct((rows, width), jnp.bfloat16),
         in_specs=[pl.BlockSpec(memory_space=pltpu.VMEM)] * 2,
         out_specs=pl.BlockSpec(memory_space=pltpu.VMEM),
         scratch_shapes=[
+            pltpu.VMEM((n, rows, depth), jnp.float32),
+            pltpu.VMEM((n * rows, depth), jnp.float32),
             pltpu.VMEM((CHUNKS, 2, 2, quarter, cols), jnp.float32),
             pltpu.VMEM((CHUNKS, 2, quarter, cols), jnp.float32),
             pltpu.VMEM((CHUNKS, quarter, cols), jnp.float32),
             pltpu.VMEM((CHUNKS, outer, rows, cols), jnp.float32),
             pltpu.VMEM((CHUNKS, outer, rows, cols), jnp.float32),
+            pltpu.SemaphoreType.DMA((n,)),
+            pltpu.SemaphoreType.DMA((n,)),
             pltpu.SemaphoreType.DMA((CHUNKS,)),
             pltpu.SemaphoreType.DMA((CHUNKS,)),
             pltpu.SemaphoreType.DMA((CHUNKS,)),
@@ -183,7 +263,7 @@
         compiler_params=pltpu.CompilerParams(
             collective_id=1, has_side_effects=True, vmem_limit_bytes=VMEM_LIMIT
         ),
-    )(ordered.reshape(total_rows, depth), weight)
+    )(heads, weight)
 
 
 def rotate(values_in, places):
@@ -237,7 +317,7 @@
         context
         + own_weight.astype(jnp.float32)[..., None] * new_values.astype(jnp.float32)[:, :, None, :]
     )
-    return context.astype(jnp.bfloat16).reshape(row_count, head_count * HEAD_WIDTH)
+    return context.reshape(row_count, head_count * HEAD_WIDTH)
 
 
 def on_device(
@@ -286,7 +366,7 @@
     terms = jnp.dot(masked_low, up_factor_rows, preferred_element_type=jnp.float32)
     packed = jnp.concatenate([query_part, kv_part, terms], axis=1)
     packed = packed.reshape(tp, piece_rows // tp, packed.shape[1])
-    received = lax.all_to_all(packed, "tp", split_axis=0, concat_axis=0, tiled=True)
+    received = exchange(packed, tp)
     own_rows = piece_rows // tp
     plain_query = jnp.transpose(received[:, :, :query_cols], (1, 0, 2)).reshape(own_rows, -1)
     row_keyval = (
@@ -299,8 +379,8 @@
         jnp.bfloat16
     )
     context = attend(row_query, row_keyval, cached_key_rows, cached_value_rows, cached_length_rows)
-    head_context = lax.all_to_all(context, "tp", split_axis=1, concat_axis=0, tiled=True)
-    return project_and_scatter(head_context, output_weight, tp)
+    heads = jnp.transpose(context.reshape(own_rows, tp, -1), (1, 0, 2))
+    return project_and_scatter(heads, output_weight, tp)
 
 
 def solution(mesh):

time: 63.3 us -> 56.5 us (0.89)
  Pallas kernels: 28.2 us -> 45.7 us
  waiting for transfers between devices: 10.4 us -> 0 us
  blocking collectives: 9.32 us -> 0 us
  starting transfers between devices: 4.53 us -> 0 us
  local copies, waits for them, and re-layouts: 4.61 us -> 3.92 us
  other arithmetic: 0.86 us -> 1.54 us
    all_to_all x1 -> x0, waiting for transfers between devices: 10.4 us -> none  [on_device(): lax.all_to_all(packed, 'tp', split_axis=0, concat_axis=0, tiled=True)]
    pallas_call x0 -> x1, Pallas kernels: none -> 9.88 us  [exchange(): pl.pallas_call(functools.partial(exchange_kernel, n), out_shape=jax.Shape...]
    all_to_all x1 -> x0, blocking collectives: 9.32 us -> none  [on_device(): lax.all_to_all(context, 'tp', split_axis=1, concat_axis=0, tiled=True)]
    pallas_call x1, Pallas kernels: 14.6 us -> 22.2 us  [project_and_scatter(): pl.pallas_call(functools.partial(project_kernel, n, rows), out_shape=jax....]
    all_to_all x1 -> x0, starting transfers between devices: 4.53 us -> none  [on_device(): lax.all_to_all(packed, 'tp', split_axis=0, concat_axis=0, tiled=True)]
    dot_general x1, matrix products: 1.57 us -> 0.5 us  [attend(): jnp.einsum('rgqd,rcgd->rgqc', grouped, old_keys, preferred_element_type=j...]
    dot_general x1, matrix products: 0.31 us -> 1.35 us  [attend(): jnp.einsum('rgqc,rcgd->rgqd', weights, old_values, preferred_element_type...]
    reshape x1, local copies, waits for them, and re-layouts: 0.88 us -> 0.17 us  [on_device(): packed = packed.reshape(tp, piece_rows // tp, packed.shape[1])]
  transfers between devices with their start and end apart: 1 -> 0, of which waited for: 1 -> 0; matrix products, arithmetic and copies ran while one was open for 0% -> 0% of each run, Pallas kernels for 0% -> 0%
where the time goes in v2:
time: 56.5 us; the launch traced here: 56.2 us
  Pallas kernels  45.7 us (81%)
  matrix products  4.81 us (9%)
  local copies, waits for them, and re-layouts  3.92 us (7%)
  other arithmetic  1.54 us (3%)
    pallas_call x1, Pallas kernels, project_and_scatter(): pl.pallas_call(functools.partial(project_kernel, n, rows), out_shape=jax....  22.2 us
    pallas_call x1, Pallas kernels, normalize_and_gather(): pl.pallas_call(functools.partial(gather_kernel, n, width), out_shape=jax....  13.6 us
    pallas_call x1, Pallas kernels, exchange(): pl.pallas_call(functools.partial(exchange_kernel, n), out_shape=jax.Shape...  9.88 us
    dot_general x1, matrix products, on_device(): jnp.dot(masked_low, up_factor_rows, preferred_element_type=jnp.float32)  1.88 us
    unnamed x11, local copies, waits for them, and re-layouts  1.77 us
    dot_general x1, matrix products, attend(): jnp.einsum('rgqc,rcgd->rgqd', weights, old_values, preferred_element_type...  1.35 us

profile of v2, /device:TPU:0, one launch (start us, length us, event | category | flops | bytes accessed | tf_op | source)
XLA Modules:
  0.0 56.2 jit_solution(586000164196862020)
XLA Ops:
  0.0 0.0 copy-start
  0.0 0.9 %reshape.145.x_ref = bf16[16,1024]{1,0:T(8,128)(2,1)S(1)} reshape(bf16[2,8192]{1,0:T(2,128)(2,1)} %param.12) | data formatting | bytes 65536 | tf_op jit(solution)/shard_map/reshape | solution.py:110
  0.9 0.8 %reshape.146.gain_ref = f32[8,1024]{1,0:T(8,128)S(1)} reshape(f32[8192]{0:T(1024)} %param.13) | data formatting | bytes 65536 | tf_op jit(solution)/shard_map/reshape | solution.py:110
  1.7 13.6 %shard_map.118 = bf16[16,16,1024]{2,1,0:T(8,128)(2,1)S(1)} custom-call(bf16[16,1024]{1,0:T(8,128)(2,1)S(1)} %reshape.145.x_ref, f32[8,1024]{1,0:T(8,128)S(1)} %reshape.146.gain_ref), custom_call_target="tpu_custom_call" | custom-call | tf_op jit(solution)/shard_map/pallas_call | solution.py:96
  15.3 0.2 reshape.147
  15.6 0.8 %select_reduce_fusion = s32[32]{0:T(128)S(1)} fusion(s32[16]{0:T(128)} %param.23, s32[32]{0:T(128)} %param.21), kind=kLoop, calls=%fused_computation.35 | loop fusion | flops 1504 | bytes 320 | tf_op jit(solution)/shard_map/reduce_sum | solution.py:344
  16.4 1.9 %fusion.2 = f32[32,2048]{1,0:T(8,128)S(1)} fusion(bf16[32,8192]{1,0:T(8,128)(2,1)S(1)} %reshape.147, bf16[1,8192,64]{1,2,0:T(8,128)(2,1)} %param.17, bf16[1,64,2048]{2,1,0:T(8,128)(2,1)} %param.18, pred[32]{0:T(512)(128)(4,1)S(1)} %broadcast_compare_fusion), kind=kOutput, calls=%fused_computation.5 | convolution fusion | flops 41947136 | bytes 2097184 | tf_op jit(solution)/shard_map/dot_general | solution.py:366
  18.2 0.0 copy-done
  18.2 0.0 copy-start.2
  18.3 0.4 fusion.25
  18.7 1.1 %copy-done.2 = bf16[8192,128]{1,0:T(8,128)(2,1)S(1)} copy-done((bf16[8192,128]{1,0:T(8,128)(2,1)S(1)}, bf16[8192,128]{1,0:T(8,128)(2,1)}, u32[]{:S(2)}) %copy-start.2) | copy-done | bytes 2097176
  19.8 0.0 copy-start.4
  19.8 0.4 fusion.26
  20.3 0.0 copy-start.3
  20.3 0.2 reshape.149.packed_ref
  20.5 0.0 copy-start.1
  20.5 9.9 %shard_map.119 = f32[16,2,2304]{2,1,0:T(2,128)S(1)} custom-call(f32[16,2,2304]{2,1,0:T(2,128)S(1)} %reshape.149.packed_ref), custom_call_target="tpu_custom_call" | custom-call | tf_op jit(solution)/shard_map/pallas_call | solution.py:140
  30.5 0.0 copy-done.4
  30.5 0.1 multiply_cosine_fusion
  30.6 0.1 subtract_convert_fusion.1
  30.7 0.1 maximum_bitcast_fusion
  30.8 0.1 slice_reduce_fusion
  30.9 0.1 subtract_convert_fusion
  31.0 0.2 fusion.18
  31.2 0.1 iota_compare_fusion.1
  31.3 0.0 copy-done.3
  31.3 0.5 fusion.24
  31.8 0.2 fusion.12
  32.0 1.3 %convolution_add_fusion = f32[2,8,2,128]{3,2,1,0:T(2,128)S(1)} fusion(f32[2,8,2,128]{3,2,1,0:T(2,128)S(1)} %get-tuple-element.16, f32[2,8,128]{2,1,0:T(8,128)S(1)} %get-tuple-element.17, f32[2,8,2]{2,1,0:T(8,128)S(1)} %get-tuple-element.6, f32[2,8,2]{2,1,0:T(8,128)S(1)} %get-tuple-element.5, f32[2,8,2]{2,1,0:T(8,128)S(1)} %multiply_maximum_fusion, ...), kind=kOutput, calls=%fused_computation | convolution fusion | flops 1069056 | bytes 565632 | tf_op jit(solution)/shard_map/rgqc,rcgd->rgqd/dot_general | solution.py:315
  33.4 0.0 copy-done.1
  33.4 22.2 %shard_map.120 = bf16[2,8192]{1,0:T(2,128)(2,1)S(1)} custom-call(f32[16,2,128]{2,1,0:T(2,128)S(1)} %bitcast.61, bf16[128,8192]{1,0:T(8,128)(2,1)S(1)} %copy-done.1), custom_call_target="tpu_custom_call" | custom-call | tf_op jit(solution)/shard_map/pallas_call | solution.py:241
  55.6 0.6 %copy.44 = bf16[2,8192]{1,0:T(2,128)(2,1)} copy(bf16[2,8192]{1,0:T(2,128)(2,1)S(1)} %shard_map.120) | data formatting | bytes 65536
  (13 shorter events, 0.1 us)
Async XLA Ops:
  0.0 18.2 %copy-start = (bf16[8192,128]{1,0:T(8,128)(2,1)S(1)}, bf16[8192,128]{1,0:T(8,128)(2,1)}, u32[]{:S(2)}) copy-start(bf16[8192,128]{1,0:T(8,128)(2,1)} %param.14) | copy-start | bytes 6291460
  18.2 1.6 %copy-start.2 = (bf16[8192,128]{1,0:T(8,128)(2,1)S(1)}, bf16[8192,128]{1,0:T(8,128)(2,1)}, u32[]{:S(2)}) copy-start(bf16[8192,128]{1,0:T(8,128)(2,1)} %param.15) | copy-start | bytes 6291460
  19.8 10.6 %copy-start.4 = (s32[2]{0:T(128)S(1)}, s32[2]{0:T(128)}, u32[]{:S(2)}) copy-start(s32[2]{0:T(128)} %param.22) | copy-start | bytes 28
  20.3 11.0 %copy-start.3 = (bf16[2,128,1024]{2,1,0:T(8,128)(2,1)S(1)}, bf16[2,128,1024]{2,1,0:T(8,128)(2,1)}, u32[]{:S(2)}) copy-start(bf16[2,128,1024]{2,1,0:T(8,128)(2,1)} %param.19) | copy-start | bytes 1572868
  20.5 12.9 %copy-start.1 = (bf16[128,8192]{1,0:T(8,128)(2,1)S(1)}, bf16[128,8192]{1,0:T(8,128)(2,1)}, u32[]{:S(2)}) copy-start(bf16[128,8192]{1,0:T(8,128)(2,1)} %w_ref.1) | copy-start | bytes 6291460

commit v3 on v2

--- a/solution.py
+++ b/solution.py
@@ -21,24 +21,35 @@
 FOLD = 8
 
 
+def flip(index, bits):
+    bit = 1
+    while bit <= bits:
+        if bits & bit:
+            index = index + bit - 2 * bit * ((index // bit) % 2)
+        bit *= 2
+    return index
+
+
 def peers(n):
     me = lax.axis_index("tp")
     outer = n // 4
     a, b, c = me // 4, (me // 2) % 2, me % 2
     core_peer = a * 4 + b * 2 + (1 - c)
     mid_peer = a * 4 + (1 - b) * 2 + c
-    ahead = [((a + k) % outer) * 4 + b * 2 + c for k in range(outer)]
-    behind = [((a + outer - k) % outer) * 4 + b * 2 + c for k in range(outer)]
-    return me, outer, a, b, c, core_peer, mid_peer, ahead, behind
-
-
-def greet(partners):
+    far = [flip(a, k) * 4 + b * 2 + c for k in range(outer)]
+    return me, outer, a, b, c, core_peer, mid_peer, far
+
+
+def hail(partners):
     barrier = pltpu.get_barrier_semaphore()
     for partner in partners:
         pl.semaphore_signal(
             barrier, inc=1, device_id={"tp": partner}, device_id_type=pl.DeviceIdType.MESH
         )
-    pl.semaphore_wait(barrier, len(partners))
+
+
+def meet(partners):
+    pl.semaphore_wait(pltpu.get_barrier_semaphore(), len(partners))
 
 
 def send(src, dst, send_sem, recv_sem, target):
@@ -52,15 +63,27 @@
     )
 
 
-def gather_kernel(n, width, x_ref, gain_ref, out_ref, far_send, mid_send, core_send, recv):
-    me, outer, a, b, c, core_peer, mid_peer, ahead, behind = peers(n)
-    rows = x_ref.shape[0] // FOLD
+def gather_kernel(
+    n, x_ref, gain_ref, out_ref, x_fold, gain_fold, far_send, mid_send, core_send, recv
+):
+    me, outer, a, b, c, core_peer, mid_peer, far = peers(n)
+    partners = [core_peer, mid_peer] + far[1:]
+    hail(partners)
+    rows, width = x_ref.shape
+    fold_width = width // FOLD
+    for s in range(FOLD):
+        part = pl.ds(s * fold_width, fold_width)
+        gain_fold[pl.ds(s, 1), :] = gain_ref[:, part]
+        piece = x_ref[:, part].astype(jnp.float32)
+        for r in range(rows):
+            x_fold[pl.ds(r * FOLD + s, 1), :] = piece[r : r + 1, :]
+    normed = []
     for r in range(rows):
-        part = pl.ds(r * FOLD, FOLD)
-        x = x_ref[part, :].astype(jnp.float32)
+        x = x_fold[pl.ds(r * FOLD, FOLD), :]
         mean = jnp.sum(x * x) / width
-        out_ref[me, part, :] = (x * lax.rsqrt(mean + EPSILON) * gain_ref[...]).astype(jnp.bfloat16)
-    greet([core_peer, mid_peer] + ahead[1:])
+        normed.append(x * lax.rsqrt(mean + EPSILON) * gain_fold[...])
+    out_ref[me] = jnp.concatenate(normed, axis=0).astype(jnp.bfloat16)
+    meet(partners)
 
     def push(block, sem, target):
         copy = send(out_ref.at[block], out_ref.at[block], sem, recv.at[block], target)
@@ -70,19 +93,19 @@
     def arrived(block):
         send(out_ref.at[block], out_ref.at[block], core_send.at[0], recv.at[block], core_peer).wait_recv()
 
-    copies = [push(me, far_send.at[k], ahead[k]) for k in range(1, outer)]
-    copies.append(push(me, mid_send.at[0], mid_peer))
+    copies = [push(me, mid_send.at[0], mid_peer)]
+    copies += [push(me, far_send.at[k], far[k]) for k in range(1, outer)]
     copies.append(push(me, core_send.at[0], core_peer))
     for k in range(1, outer):
-        arrived(behind[k])
-        copies.append(push(behind[k], mid_send.at[k], mid_peer))
-        copies.append(push(behind[k], core_send.at[k], core_peer))
-    across = [behind[k] - b * 2 + (1 - b) * 2 for k in range(outer)]
+        arrived(far[k])
+        copies.append(push(far[k], mid_send.at[k], mid_peer))
+        copies.append(push(far[k], core_send.at[k], core_peer))
+    across = [far[k] - b * 2 + (1 - b) * 2 for k in range(outer)]
     for k in range(outer):
         arrived(across[k])
         copies.append(push(across[k], core_send.at[outer + k], core_peer))
     for k in range(outer):
-        arrived(behind[k] - c + (1 - c))
+        arrived(far[k] - c + (1 - c))
     for k in range(outer):
         arrived(across[k] - c + (1 - c))
     for copy in copies:
@@ -94,11 +117,13 @@
     fold_width = width // FOLD
     outer = n // 4
     gathered = pl.pallas_call(
-        functools.partial(gather_kernel, n, width),
+        functools.partial(gather_kernel, n),
         out_shape=jax.ShapeDtypeStruct((n, rows * FOLD, fold_width), jnp.bfloat16),
         in_specs=[pl.BlockSpec(memory_space=pltpu.VMEM)] * 2,
         out_specs=pl.BlockSpec(memory_space=pltpu.VMEM),
         scratch_shapes=[
+            pltpu.VMEM((rows * FOLD, fold_width), jnp.float32),
+            pltpu.VMEM((FOLD, fold_width), jnp.float32),
             pltpu.SemaphoreType.DMA((outer,)),
             pltpu.SemaphoreType.DMA((outer,)),
             pltpu.SemaphoreType.DMA((2 * outer,)),
@@ -107,20 +132,21 @@
         compiler_params=pltpu.CompilerParams(
             collective_id=0, has_side_effects=True, vmem_limit_bytes=VMEM_LIMIT
         ),
-    )(tokens.reshape(rows * FOLD, fold_width), gain.reshape(FOLD, fold_width))
+    )(tokens, gain.reshape(1, width))
     return gathered.reshape(n * rows, width)
 
 
 def others(n):
     me = lax.axis_index("tp")
-    return me, [(me + k) % n for k in range(1, n)], [(me + n - k) % n for k in range(1, n)]
+    return me, [flip(me, k) for k in range(1, n)]
 
 
 def exchange_kernel(n, packed_ref, out_ref, own_sem, send_sem, recv_sem):
-    me, to, origin = others(n)
+    me, to = others(n)
+    hail(to)
     own = pltpu.make_async_copy(packed_ref.at[me], out_ref.at[me], own_sem)
     own.start()
-    greet(to)
+    meet(to)
     copies = []
     for k in range(n - 1):
         copy = send(
@@ -132,7 +158,7 @@
     for k in range(n - 1):
         copies[k].wait_send()
         send(
-            packed_ref.at[to[k]], out_ref.at[origin[k]], send_sem.at[k], recv_sem.at[k], to[k]
+            packed_ref.at[to[k]], out_ref.at[to[k]], send_sem.at[k], recv_sem.at[k], to[k]
         ).wait_recv()
 
 
@@ -175,12 +201,13 @@
     s3,
     q3,
 ):
-    me, outer, a, b, c, core_peer, mid_peer, ahead, behind = peers(n)
+    me, outer, a, b, c, core_peer, mid_peer, far = peers(n)
     cols = w_ref.shape[1] // CHUNKS
     quarter = outer * rows
     slot = (c * 2 + b) * outer + a
-    _, to, _ = others(n)
-    greet(to)
+    _, to = others(n)
+    hail(to)
+    meet(to)
     sent = []
     for k in range(n - 1):
         copy = send(heads_ref.at[to[k]], h_ref.at[slot], s0.at[k], q0.at[slot], to[k])
@@ -188,7 +215,7 @@
         sent.append(copy)
     h_ref[slot] = heads_ref[me]
     for k in range(n - 1):
-        source = (me + n - 1 - k) % n
+        source = to[k]
         place = ((source % 2) * 2 + (source // 2) % 2) * outer + source // 4
         send(heads_ref.at[to[k]], h_ref.at[place], s0.at[k], q0.at[place], to[k]).wait_recv()
     for t in range(n):
@@ -217,7 +244,7 @@
         group = []
         for k in range(1, outer):
             copy = send(
-                x_ref.at[i, (a + k) % outer], r3.at[i, k], s3.at[i, k], q3.at[i, k], ahead[k]
+                x_ref.at[i, flip(a, k)], r3.at[i, k], s3.at[i, k], q3.at[i, k], far[k]
             )
             copy.start()
             group.append(copy)

time: 56.5 us -> 55.8 us (0.988)
  Pallas kernels: 45.7 us -> 45 us
    reshape x2 -> x0, local copies, waits for them, and re-layouts: 1.7 us -> none  [the longest x1 0.93 us: normalize_and_gather(): tokens.reshape(rows * FOLD, fold_width)]
    unnamed x11 -> x15, local copies, waits for them, and re-layouts: 1.77 us -> 3.44 us
    pallas_call x1, Pallas kernels: 22.2 us -> 20.7 us  [project_and_scatter(): pl.pallas_call(functools.partial(project_kernel, n, rows), out_shape=jax....]
    pallas_call x1, Pallas kernels: 9.88 us -> 10.9 us  [exchange(): pl.pallas_call(functools.partial(exchange_kernel, n), out_shape=jax.Shape...]
where the time goes in v3:
time: 55.8 us; the launch traced here: 55.5 us
  Pallas kernels  45 us (81%)
  matrix products  4.81 us (9%)
  local copies, waits for them, and re-layouts  3.88 us (7%)
  other arithmetic  1.54 us (3%)
    pallas_call x1, Pallas kernels, project_and_scatter(): pl.pallas_call(functools.partial(project_kernel, n, rows), out_shape=jax....  20.7 us
    pallas_call x1, Pallas kernels, normalize_and_gather(): pl.pallas_call(functools.partial(gather_kernel, n), out_shape=jax.ShapeDt...  13.5 us
    pallas_call x1, Pallas kernels, exchange(): pl.pallas_call(functools.partial(exchange_kernel, n), out_shape=jax.Shape...  10.9 us
    unnamed x15, local copies, waits for them, and re-layouts  3.44 us
    dot_general x1, matrix products, on_device(): jnp.dot(masked_low, up_factor_rows, preferred_element_type=jnp.float32)  1.88 us
    dot_general x1, matrix products, attend(): jnp.einsum('rgqc,rcgd->rgqd', weights, old_values, preferred_element_type...  1.35 us

profile of v3, /device:TPU:0, one launch (start us, length us, event | category | flops | bytes accessed | tf_op | source)
XLA Modules:
  0.0 55.5 jit_solution(16558607309185654409)
XLA Ops:
  0.0 0.0 copy-start
  0.0 0.0 copy-start.2
  0.0 0.9 %copy-done.2 = bf16[2,8192]{1,0:T(2,128)(2,1)S(1)} copy-done((bf16[2,8192]{1,0:T(2,128)(2,1)S(1)}, bf16[2,8192]{1,0:T(2,128)(2,1)}, u32[]{:S(2)}) %copy-start.2) | copy-done | bytes 32792
  0.9 0.8 %copy-done.3 = f32[8192]{0:T(1024)S(1)} copy-done((f32[8192]{0:T(1024)S(1)}, f32[8192]{0:T(1024)}, u32[]{:S(2)}) %copy-start.3) | copy-done | bytes 32792
  1.7 13.5 %shard_map.118 = bf16[16,16,1024]{2,1,0:T(8,128)(2,1)S(1)} custom-call(bf16[2,8192]{1,0:T(2,128)(2,1)S(1)} %copy-done.2, f32[1,8192]{1,0:T(1,128)S(1)} %bitcast.63), custom_call_target="tpu_custom_call" | custom-call | tf_op jit(solution)/shard_map/pallas_call | solution.py:119
  15.1 0.2 reshape.143
  15.4 0.8 %select_reduce_fusion = s32[32]{0:T(128)S(1)} fusion(s32[16]{0:T(128)} %param.23, s32[32]{0:T(128)} %param.21), kind=kLoop, calls=%fused_computation.35 | loop fusion | flops 1504 | bytes 320 | tf_op jit(solution)/shard_map/reduce_sum | solution.py:371
  16.2 1.9 %fusion.2 = f32[32,2048]{1,0:T(8,128)S(1)} fusion(bf16[32,8192]{1,0:T(8,128)(2,1)S(1)} %reshape.143, bf16[1,8192,64]{1,2,0:T(8,128)(2,1)} %param.17, bf16[1,64,2048]{2,1,0:T(8,128)(2,1)} %param.18, pred[32]{0:T(512)(128)(4,1)S(1)} %broadcast_compare_fusion), kind=kOutput, calls=%fused_computation.5 | convolution fusion | flops 41947136 | bytes 2097184 | tf_op jit(solution)/shard_map/dot_general | solution.py:393
  18.0 0.0 copy-done
  18.1 0.0 copy-start.4
  18.1 0.4 fusion.25
  18.5 1.1 %copy-done.4 = bf16[8192,128]{1,0:T(8,128)(2,1)S(1)} copy-done((bf16[8192,128]{1,0:T(8,128)(2,1)S(1)}, bf16[8192,128]{1,0:T(8,128)(2,1)}, u32[]{:S(2)}) %copy-start.4) | copy-done | bytes 2097176
  19.7 0.4 fusion.26
  20.1 0.0 copy-start.5
  20.1 0.2 reshape.145.packed_ref
  20.3 0.0 copy-start.1
  20.3 10.9 %shard_map.119 = f32[16,2,2304]{2,1,0:T(2,128)S(1)} custom-call(f32[16,2,2304]{2,1,0:T(2,128)S(1)} %reshape.145.packed_ref), custom_call_target="tpu_custom_call" | custom-call | tf_op jit(solution)/shard_map/pallas_call | solution.py:166
  31.3 0.0 copy-done.6
  31.3 0.1 multiply_cosine_fusion
  31.4 0.1 subtract_convert_fusion.1
  31.5 0.1 maximum_bitcast_fusion
  31.6 0.1 slice_reduce_fusion
  31.7 0.1 subtract_convert_fusion
  31.8 0.2 fusion.18
  32.0 0.1 iota_compare_fusion.1
  32.1 0.0 copy-done.5
  32.1 0.5 fusion.24
  32.6 0.2 fusion.12
  32.8 1.3 %convolution_add_fusion = f32[2,8,2,128]{3,2,1,0:T(2,128)S(1)} fusion(f32[2,8,2,128]{3,2,1,0:T(2,128)S(1)} %get-tuple-element.16, f32[2,8,128]{2,1,0:T(8,128)S(1)} %get-tuple-element.17, f32[2,8,2]{2,1,0:T(8,128)S(1)} %get-tuple-element.6, f32[2,8,2]{2,1,0:T(8,128)S(1)} %get-tuple-element.5, f32[2,8,2]{2,1,0:T(8,128)S(1)} %multiply_maximum_fusion, ...), kind=kOutput, calls=%fused_computation | convolution fusion | flops 1069056 | bytes 565632 | tf_op jit(solution)/shard_map/rgqc,rcgd->rgqd/dot_general | solution.py:342
  34.2 0.0 copy-done.1
  34.2 20.7 %shard_map.120 = bf16[2,8192]{1,0:T(2,128)(2,1)S(1)} custom-call(f32[16,2,128]{2,1,0:T(2,128)S(1)} %bitcast.62, bf16[128,8192]{1,0:T(8,128)(2,1)S(1)} %copy-done.1), custom_call_target="tpu_custom_call" | custom-call | tf_op jit(solution)/shard_map/pallas_call | solution.py:268
  54.9 0.6 %copy.44 = bf16[2,8192]{1,0:T(2,128)(2,1)} copy(bf16[2,8192]{1,0:T(2,128)(2,1)S(1)} %shard_map.120) | data formatting | bytes 65536
  (15 shorter events, 0.1 us)
Async XLA Ops:
  0.0 18.0 %copy-start = (bf16[8192,128]{1,0:T(8,128)(2,1)S(1)}, bf16[8192,128]{1,0:T(8,128)(2,1)}, u32[]{:S(2)}) copy-start(bf16[8192,128]{1,0:T(8,128)(2,1)} %param.14) | copy-start | bytes 6291460
  0.0 0.9 %copy-start.2 = (bf16[2,8192]{1,0:T(2,128)(2,1)S(1)}, bf16[2,8192]{1,0:T(2,128)(2,1)}, u32[]{:S(2)}) copy-start(bf16[2,8192]{1,0:T(2,128)(2,1)} %x_ref.1) | copy-start | bytes 98308
  0.9 0.8 %copy-start.3 = (f32[8192]{0:T(1024)S(1)}, f32[8192]{0:T(1024)}, u32[]{:S(2)}) copy-start(f32[8192]{0:T(1024)} %param.13) | copy-start | bytes 98308
  18.1 1.6 %copy-start.4 = (bf16[8192,128]{1,0:T(8,128)(2,1)S(1)}, bf16[8192,128]{1,0:T(8,128)(2,1)}, u32[]{:S(2)}) copy-start(bf16[8192,128]{1,0:T(8,128)(2,1)} %param.15) | copy-start | bytes 6291460
  19.7 11.6 %copy-start.6 = (s32[2]{0:T(128)S(1)}, s32[2]{0:T(128)}, u32[]{:S(2)}) copy-start(s32[2]{0:T(128)} %param.22) | copy-start | bytes 28
  20.1 12.0 %copy-start.5 = (bf16[2,128,1024]{2,1,0:T(8,128)(2,1)S(1)}, bf16[2,128,1024]{2,1,0:T(8,128)(2,1)}, u32[]{:S(2)}) copy-start(bf16[2,128,1024]{2,1,0:T(8,128)(2,1)} %param.19) | copy-start | bytes 1572868
  20.3 13.9 %copy-start.1 = (bf16[128,8192]{1,0:T(8,128)(2,1)S(1)}, bf16[128,8192]{1,0:T(8,128)(2,1)}, u32[]{:S(2)}) copy-start(bf16[128,8192]{1,0:T(8,128)(2,1)} %w_ref.1) | copy-start | bytes 6291460

commit v4 on v3

--- a/solution.py
+++ b/solution.py
@@ -17,7 +17,7 @@
 ROPE_BASE = 500000.0
 
 VMEM_LIMIT = 24 * 1024 * 1024
-CHUNKS = 4
+CHUNKS = 8
 FOLD = 8
 
 
@@ -64,19 +64,23 @@
 
 
 def gather_kernel(
-    n, x_ref, gain_ref, out_ref, x_fold, gain_fold, far_send, mid_send, core_send, recv
+    n, x_ref, gain_hbm, out_ref, gain_ref, x_fold, gain_fold, load, far_send, mid_send, core_send, recv
 ):
     me, outer, a, b, c, core_peer, mid_peer, far = peers(n)
     partners = [core_peer, mid_peer] + far[1:]
+    fetch = pltpu.make_async_copy(gain_hbm, gain_ref, load)
+    fetch.start()
     hail(partners)
     rows, width = x_ref.shape
     fold_width = width // FOLD
     for s in range(FOLD):
         part = pl.ds(s * fold_width, fold_width)
-        gain_fold[pl.ds(s, 1), :] = gain_ref[:, part]
         piece = x_ref[:, part].astype(jnp.float32)
         for r in range(rows):
             x_fold[pl.ds(r * FOLD + s, 1), :] = piece[r : r + 1, :]
+    fetch.wait()
+    for s in range(FOLD):
+        gain_fold[pl.ds(s, 1), :] = gain_ref[:, pl.ds(s * fold_width, fold_width)]
     normed = []
     for r in range(rows):
         x = x_fold[pl.ds(r * FOLD, FOLD), :]
@@ -119,11 +123,13 @@
     gathered = pl.pallas_call(
         functools.partial(gather_kernel, n),
         out_shape=jax.ShapeDtypeStruct((n, rows * FOLD, fold_width), jnp.bfloat16),
-        in_specs=[pl.BlockSpec(memory_space=pltpu.VMEM)] * 2,
+        in_specs=[pl.BlockSpec(memory_space=pltpu.VMEM), pl.BlockSpec(memory_space=pl.ANY)],
         out_specs=pl.BlockSpec(memory_space=pltpu.VMEM),
         scratch_shapes=[
+            pltpu.VMEM((1, width), jnp.float32),
             pltpu.VMEM((rows * FOLD, fold_width), jnp.float32),
             pltpu.VMEM((FOLD, fold_width), jnp.float32),
+            pltpu.SemaphoreType.DMA(()),
             pltpu.SemaphoreType.DMA((outer,)),
             pltpu.SemaphoreType.DMA((outer,)),
             pltpu.SemaphoreType.DMA((2 * outer,)),

time: 55.8 us -> 55.8 us (level)
  no operation moved by 1% of the time
where the time goes in v4:
time: 55.8 us; the launch traced here: 55.6 us
  Pallas kernels  45.1 us (81%)
  matrix products  4.81 us (9%)
  local copies, waits for them, and re-layouts  3.88 us (7%)
  other arithmetic  1.54 us (3%)
    pallas_call x1, Pallas kernels, project_and_scatter(): pl.pallas_call(functools.partial(project_kernel, n, rows), out_shape=jax....  20.7 us
    pallas_call x1, Pallas kernels, normalize_and_gather(): pl.pallas_call(functools.partial(gather_kernel, n), out_shape=jax.ShapeDt...  13.5 us
    pallas_call x1, Pallas kernels, exchange(): pl.pallas_call(functools.partial(exchange_kernel, n), out_shape=jax.Shape...  10.9 us
    unnamed x15, local copies, waits for them, and re-layouts  3.44 us
    dot_general x1, matrix products, on_device(): jnp.dot(masked_low, up_factor_rows, preferred_element_type=jnp.float32)  1.88 us
    dot_general x1, matrix products, attend(): jnp.einsum('rgqc,rcgd->rgqd', weights, old_values, preferred_element_type...  1.35 us

profile of v4, /device:TPU:0, one launch (start us, length us, event | category | flops | bytes accessed | tf_op | source)
XLA Modules:
  0.0 55.6 jit_solution(10131333368433597392)
XLA Ops:
  0.0 0.0 copy-start
  0.0 0.0 copy-start.2
  0.0 0.9 %copy-done.2 = bf16[2,8192]{1,0:T(2,128)(2,1)S(1)} copy-done((bf16[2,8192]{1,0:T(2,128)(2,1)S(1)}, bf16[2,8192]{1,0:T(2,128)(2,1)}, u32[]{:S(2)}) %copy-start.2) | copy-done | bytes 32792
  0.9 0.8 %copy-done.3 = f32[8192]{0:T(1024)S(1)} copy-done((f32[8192]{0:T(1024)S(1)}, f32[8192]{0:T(1024)}, u32[]{:S(2)}) %copy-start.3) | copy-done | bytes 32792
  1.7 13.5 %shard_map.118 = bf16[16,16,1024]{2,1,0:T(8,128)(2,1)S(1)} custom-call(bf16[2,8192]{1,0:T(2,128)(2,1)S(1)} %copy-done.2, f32[1,8192]{1,0:T(1,128)S(1)} %bitcast.63), custom_call_target="tpu_custom_call" | custom-call | tf_op jit(solution)/shard_map/pallas_call | solution.py:123
  15.2 0.2 reshape.143
  15.4 0.8 %select_reduce_fusion = s32[32]{0:T(128)S(1)} fusion(s32[16]{0:T(128)} %param.23, s32[32]{0:T(128)} %param.21), kind=kLoop, calls=%fused_computation.35 | loop fusion | flops 1504 | bytes 320 | tf_op jit(solution)/shard_map/reduce_sum | solution.py:377
  16.2 1.9 %fusion.2 = f32[32,2048]{1,0:T(8,128)S(1)} fusion(bf16[32,8192]{1,0:T(8,128)(2,1)S(1)} %reshape.143, bf16[1,8192,64]{1,2,0:T(8,128)(2,1)} %param.17, bf16[1,64,2048]{2,1,0:T(8,128)(2,1)} %param.18, pred[32]{0:T(512)(128)(4,1)S(1)} %broadcast_compare_fusion), kind=kOutput, calls=%fused_computation.5 | convolution fusion | flops 41947136 | bytes 2097184 | tf_op jit(solution)/shard_map/dot_general | solution.py:399
  18.1 0.0 copy-done
  18.1 0.0 copy-start.4
  18.1 0.4 fusion.25
  18.6 1.1 %copy-done.4 = bf16[8192,128]{1,0:T(8,128)(2,1)S(1)} copy-done((bf16[8192,128]{1,0:T(8,128)(2,1)S(1)}, bf16[8192,128]{1,0:T(8,128)(2,1)}, u32[]{:S(2)}) %copy-start.4) | copy-done | bytes 2097176
  19.7 0.4 fusion.26
  20.1 0.0 copy-start.5
  20.2 0.2 reshape.145.packed_ref
  20.4 0.0 copy-start.1
  20.4 10.9 %shard_map.119 = f32[16,2,2304]{2,1,0:T(2,128)S(1)} custom-call(f32[16,2,2304]{2,1,0:T(2,128)S(1)} %reshape.145.packed_ref), custom_call_target="tpu_custom_call" | custom-call | tf_op jit(solution)/shard_map/pallas_call | solution.py:172
  31.3 0.0 copy-done.6
  31.3 0.1 multiply_cosine_fusion
  31.5 0.1 subtract_convert_fusion.1
  31.5 0.1 maximum_bitcast_fusion
  31.6 0.1 slice_reduce_fusion
  31.7 0.1 subtract_convert_fusion
  31.8 0.2 fusion.18
  32.0 0.1 iota_compare_fusion.1
  32.1 0.0 copy-done.5
  32.1 0.5 fusion.24
  32.6 0.2 fusion.12
  32.8 1.3 %convolution_add_fusion = f32[2,8,2,128]{3,2,1,0:T(2,128)S(1)} fusion(f32[2,8,2,128]{3,2,1,0:T(2,128)S(1)} %get-tuple-element.16, f32[2,8,128]{2,1,0:T(8,128)S(1)} %get-tuple-element.17, f32[2,8,2]{2,1,0:T(8,128)S(1)} %get-tuple-element.6, f32[2,8,2]{2,1,0:T(8,128)S(1)} %get-tuple-element.5, f32[2,8,2]{2,1,0:T(8,128)S(1)} %multiply_maximum_fusion, ...), kind=kOutput, calls=%fused_computation | convolution fusion | flops 1069056 | bytes 565632 | tf_op jit(solution)/shard_map/rgqc,rcgd->rgqd/dot_general | solution.py:348
  34.2 0.0 copy-done.1
  34.2 20.7 %shard_map.120 = bf16[2,8192]{1,0:T(2,128)(2,1)S(1)} custom-call(f32[16,2,128]{2,1,0:T(2,128)S(1)} %bitcast.62, bf16[128,8192]{1,0:T(8,128)(2,1)S(1)} %copy-done.1), custom_call_target="tpu_custom_call" | custom-call | tf_op jit(solution)/shard_map/pallas_call | solution.py:274
  55.0 0.6 %copy.44 = bf16[2,8192]{1,0:T(2,128)(2,1)} copy(bf16[2,8192]{1,0:T(2,128)(2,1)S(1)} %shard_map.120) | data formatting | bytes 65536
  (15 shorter events, 0.1 us)
Async XLA Ops:
  0.0 18.1 %copy-start = (bf16[8192,128]{1,0:T(8,128)(2,1)S(1)}, bf16[8192,128]{1,0:T(8,128)(2,1)}, u32[]{:S(2)}) copy-start(bf16[8192,128]{1,0:T(8,128)(2,1)} %param.14) | copy-start | bytes 6291460
  0.0 0.9 %copy-start.2 = (bf16[2,8192]{1,0:T(2,128)(2,1)S(1)}, bf16[2,8192]{1,0:T(2,128)(2,1)}, u32[]{:S(2)}) copy-start(bf16[2,8192]{1,0:T(2,128)(2,1)} %x_ref.1) | copy-start | bytes 98308
  0.9 0.8 %copy-start.3 = (f32[8192]{0:T(1024)S(1)}, f32[8192]{0:T(1024)}, u32[]{:S(2)}) copy-start(f32[8192]{0:T(1024)} %param.13) | copy-start | bytes 98308
  18.1 1.6 %copy-start.4 = (bf16[8192,128]{1,0:T(8,128)(2,1)S(1)}, bf16[8192,128]{1,0:T(8,128)(2,1)}, u32[]{:S(2)}) copy-start(bf16[8192,128]{1,0:T(8,128)(2,1)} %param.15) | copy-start | bytes 6291460
  19.7 11.6 %copy-start.6 = (s32[2]{0:T(128)S(1)}, s32[2]{0:T(128)}, u32[]{:S(2)}) copy-start(s32[2]{0:T(128)} %param.22) | copy-start | bytes 28
  20.1 12.0 %copy-start.5 = (bf16[2,128,1024]{2,1,0:T(8,128)(2,1)S(1)}, bf16[2,128,1024]{2,1,0:T(8,128)(2,1)}, u32[]{:S(2)}) copy-start(bf16[2,128,1024]{2,1,0:T(8,128)(2,1)} %param.19) | copy-start | bytes 1572868
  20.4 13.9 %copy-start.1 = (bf16[128,8192]{1,0:T(8,128)(2,1)S(1)}, bf16[128,8192]{1,0:T(8,128)(2,1)}, u32[]{:S(2)}) copy-start(bf16[128,8192]{1,0:T(8,128)(2,1)} %w_ref.1) | copy-start | bytes 6291460

commit v5 on v4

--- a/solution.py
+++ b/solution.py
@@ -123,7 +123,7 @@
     gathered = pl.pallas_call(
         functools.partial(gather_kernel, n),
         out_shape=jax.ShapeDtypeStruct((n, rows * FOLD, fold_width), jnp.bfloat16),
-        in_specs=[pl.BlockSpec(memory_space=pltpu.VMEM), pl.BlockSpec(memory_space=pl.ANY)],
+        in_specs=[pl.BlockSpec(memory_space=pltpu.VMEM), pl.BlockSpec(memory_space=pltpu.HBM)],
         out_specs=pl.BlockSpec(memory_space=pltpu.VMEM),
         scratch_shapes=[
             pltpu.VMEM((1, width), jnp.float32),

time: 55.8 us -> 55.8 us (level)
  no operation moved by 1% of the time
where the time goes in v5:
time: 55.8 us; the launch traced here: 55.6 us
  Pallas kernels  45.1 us (81%)
  matrix products  4.81 us (9%)
  local copies, waits for them, and re-layouts  3.88 us (7%)
  other arithmetic  1.54 us (3%)
    pallas_call x1, Pallas kernels, project_and_scatter(): pl.pallas_call(functools.partial(project_kernel, n, rows), out_shape=jax....  20.7 us
    pallas_call x1, Pallas kernels, normalize_and_gather(): pl.pallas_call(functools.partial(gather_kernel, n), out_shape=jax.ShapeDt...  13.5 us
    pallas_call x1, Pallas kernels, exchange(): pl.pallas_call(functools.partial(exchange_kernel, n), out_shape=jax.Shape...  10.9 us
    unnamed x15, local copies, waits for them, and re-layouts  3.44 us
    dot_general x1, matrix products, on_device(): jnp.dot(masked_low, up_factor_rows, preferred_element_type=jnp.float32)  1.88 us
    dot_general x1, matrix products, attend(): jnp.einsum('rgqc,rcgd->rgqd', weights, old_values, preferred_element_type...  1.35 us

profile of v5, /device:TPU:0, one launch (start us, length us, event | category | flops | bytes accessed | tf_op | source)
XLA Modules:
  0.0 55.6 jit_solution(10131333368433597392)
XLA Ops:
  0.0 0.0 copy-start
  0.0 0.0 copy-start.2
  0.0 0.9 %copy-done.2 = bf16[2,8192]{1,0:T(2,128)(2,1)S(1)} copy-done((bf16[2,8192]{1,0:T(2,128)(2,1)S(1)}, bf16[2,8192]{1,0:T(2,128)(2,1)}, u32[]{:S(2)}) %copy-start.2) | copy-done | bytes 32792
  0.9 0.8 %copy-done.3 = f32[8192]{0:T(1024)S(1)} copy-done((f32[8192]{0:T(1024)S(1)}, f32[8192]{0:T(1024)}, u32[]{:S(2)}) %copy-start.3) | copy-done | bytes 32792
  1.7 13.5 %shard_map.118 = bf16[16,16,1024]{2,1,0:T(8,128)(2,1)S(1)} custom-call(bf16[2,8192]{1,0:T(2,128)(2,1)S(1)} %copy-done.2, f32[1,8192]{1,0:T(1,128)S(1)} %bitcast.63), custom_call_target="tpu_custom_call" | custom-call | tf_op jit(solution)/shard_map/pallas_call | solution.py:123
  15.2 0.2 reshape.143
  15.4 0.8 %select_reduce_fusion = s32[32]{0:T(128)S(1)} fusion(s32[16]{0:T(128)} %param.23, s32[32]{0:T(128)} %param.21), kind=kLoop, calls=%fused_computation.35 | loop fusion | flops 1504 | bytes 320 | tf_op jit(solution)/shard_map/reduce_sum | solution.py:377
  16.2 1.9 %fusion.2 = f32[32,2048]{1,0:T(8,128)S(1)} fusion(bf16[32,8192]{1,0:T(8,128)(2,1)S(1)} %reshape.143, bf16[1,8192,64]{1,2,0:T(8,128)(2,1)} %param.17, bf16[1,64,2048]{2,1,0:T(8,128)(2,1)} %param.18, pred[32]{0:T(512)(128)(4,1)S(1)} %broadcast_compare_fusion), kind=kOutput, calls=%fused_computation.5 | convolution fusion | flops 41947136 | bytes 2097184 | tf_op jit(solution)/shard_map/dot_general | solution.py:399
  18.1 0.0 copy-done
  18.1 0.0 copy-start.4
  18.1 0.4 fusion.25
  18.6 1.1 %copy-done.4 = bf16[8192,128]{1,0:T(8,128)(2,1)S(1)} copy-done((bf16[8192,128]{1,0:T(8,128)(2,1)S(1)}, bf16[8192,128]{1,0:T(8,128)(2,1)}, u32[]{:S(2)}) %copy-start.4) | copy-done | bytes 2097176
  19.7 0.4 fusion.26
  20.1 0.0 copy-start.5
  20.2 0.2 reshape.145.packed_ref
  20.4 0.0 copy-start.1
  20.4 10.9 %shard_map.119 = f32[16,2,2304]{2,1,0:T(2,128)S(1)} custom-call(f32[16,2,2304]{2,1,0:T(2,128)S(1)} %reshape.145.packed_ref), custom_call_target="tpu_custom_call" | custom-call | tf_op jit(solution)/shard_map/pallas_call | solution.py:172
  31.3 0.0 copy-done.6
  31.3 0.1 multiply_cosine_fusion
  31.5 0.1 subtract_convert_fusion.1
  31.5 0.1 maximum_bitcast_fusion
  31.6 0.1 slice_reduce_fusion
  31.7 0.1 subtract_convert_fusion
  31.8 0.2 fusion.18
  32.0 0.1 iota_compare_fusion.1
  32.1 0.0 copy-done.5
  32.1 0.5 fusion.24
  32.6 0.2 fusion.12
  32.8 1.3 %convolution_add_fusion = f32[2,8,2,128]{3,2,1,0:T(2,128)S(1)} fusion(f32[2,8,2,128]{3,2,1,0:T(2,128)S(1)} %get-tuple-element.16, f32[2,8,128]{2,1,0:T(8,128)S(1)} %get-tuple-element.17, f32[2,8,2]{2,1,0:T(8,128)S(1)} %get-tuple-element.6, f32[2,8,2]{2,1,0:T(8,128)S(1)} %get-tuple-element.5, f32[2,8,2]{2,1,0:T(8,128)S(1)} %multiply_maximum_fusion, ...), kind=kOutput, calls=%fused_computation | convolution fusion | flops 1069056 | bytes 565632 | tf_op jit(solution)/shard_map/rgqc,rcgd->rgqd/dot_general | solution.py:348
  34.2 0.0 copy-done.1
  34.2 20.7 %shard_map.120 = bf16[2,8192]{1,0:T(2,128)(2,1)S(1)} custom-call(f32[16,2,128]{2,1,0:T(2,128)S(1)} %bitcast.62, bf16[128,8192]{1,0:T(8,128)(2,1)S(1)} %copy-done.1), custom_call_target="tpu_custom_call" | custom-call | tf_op jit(solution)/shard_map/pallas_call | solution.py:274
  55.0 0.6 %copy.44 = bf16[2,8192]{1,0:T(2,128)(2,1)} copy(bf16[2,8192]{1,0:T(2,128)(2,1)S(1)} %shard_map.120) | data formatting | bytes 65536
  (15 shorter events, 0.1 us)
Async XLA Ops:
  0.0 18.1 %copy-start = (bf16[8192,128]{1,0:T(8,128)(2,1)S(1)}, bf16[8192,128]{1,0:T(8,128)(2,1)}, u32[]{:S(2)}) copy-start(bf16[8192,128]{1,0:T(8,128)(2,1)} %param.14) | copy-start | bytes 6291460
  0.0 0.9 %copy-start.2 = (bf16[2,8192]{1,0:T(2,128)(2,1)S(1)}, bf16[2,8192]{1,0:T(2,128)(2,1)}, u32[]{:S(2)}) copy-start(bf16[2,8192]{1,0:T(2,128)(2,1)} %x_ref.1) | copy-start | bytes 98308
  0.9 0.8 %copy-start.3 = (f32[8192]{0:T(1024)S(1)}, f32[8192]{0:T(1024)}, u32[]{:S(2)}) copy-start(f32[8192]{0:T(1024)} %param.13) | copy-start | bytes 98308
  18.1 1.6 %copy-start.4 = (bf16[8192,128]{1,0:T(8,128)(2,1)S(1)}, bf16[8192,128]{1,0:T(8,128)(2,1)}, u32[]{:S(2)}) copy-start(bf16[8192,128]{1,0:T(8,128)(2,1)} %param.15) | copy-start | bytes 6291460
  19.7 11.6 %copy-start.6 = (s32[2]{0:T(128)S(1)}, s32[2]{0:T(128)}, u32[]{:S(2)}) copy-start(s32[2]{0:T(128)} %param.22) | copy-start | bytes 28
  20.1 12.0 %copy-start.5 = (bf16[2,128,1024]{2,1,0:T(8,128)(2,1)S(1)}, bf16[2,128,1024]{2,1,0:T(8,128)(2,1)}, u32[]{:S(2)}) copy-start(bf16[2,128,1024]{2,1,0:T(8,128)(2,1)} %param.19) | copy-start | bytes 1572868
  20.4 13.9 %copy-start.1 = (bf16[128,8192]{1,0:T(8,128)(2,1)S(1)}, bf16[128,8192]{1,0:T(8,128)(2,1)}, u32[]{:S(2)}) copy-start(bf16[128,8192]{1,0:T(8,128)(2,1)} %w_ref.1) | copy-start | bytes 6291460
